TPU v7x, 128 devices: a whole 4x4x4 slice. The times are simulated.
128 devices in a mesh: row: 16 (over x_lo, y, core), col: 8 (over z, x_hi).
Axes of the slice: x: 4 (x_hi: 2, x_lo: 2; x = x_hi * 2 + x_lo), y: 4, z: 4, core: 2. Of those that a mesh axis runs over, the one named last changes fastest.
Arguments:
- pair_elements: float32 [2, 1024, 20480], P(None, ('row', 'col')), may hold values from -24 to 24
- screened_w: float32 [20480, 20480], P('row', 'col'), may hold values from -0.0390625 to 0.0390625
- occupied: int32 [1024], P('row'), may hold values 0 or 1
- freq_index: int32 [1], replicated, may hold values from 0 to 15
Outputs:
- screened_pairs: float32 [2, 1024, 20480], P(None, 'row', 'col')
- sigma_bands: float32 [2, 1024], P(None, 'row')
All inputs are finite; a program needn't handle non-finite values. No bound on the sum of `occupied` on one device may be relied on, other than what follows from the above.
Results may differ from a plain program's by a relative error of at most 0.000092.
Values sent between devices are 32-bit elements; how exact they have to be, the bound alone decides.
No kernel may reach another device: no remote copies, remote signals or barrier semaphores. Data moves between devices by JAX's collectives and lax.ppermute only.
A program may use at most 192 MiB of HBM per device.

v0:
```python
import jax
import jax.numpy as jnp
from jax import lax
from jax.sharding import PartitionSpec as P

NG = 20480


def apply_screen(block, tile):
    return jnp.einsum(
        "kbg,gh->kbh",
        block,
        tile,
        precision=lax.Precision.HIGHEST,
        preferred_element_type=jnp.float32,
    )


def per_device(pair_elements, screened_w, occupied, freq_index):
    row_count = lax.axis_size("row")
    kinds, local_bands, width_all = pair_elements.shape
    width = screened_w.shape[1]
    gathered = lax.all_gather(pair_elements, "col", axis=1, tiled=True)
    partial_terms = apply_screen(
        lax.all_to_all(gathered, "row", split_axis=2, concat_axis=1, tiled=True), screened_w
    )
    group_rows = partial_terms.shape[1] // row_count
    grouped = partial_terms.reshape(kinds, row_count, group_rows, width)
    screened = lax.psum_scatter(grouped, "row", scatter_dimension=1, tiled=True).reshape(
        kinds, group_rows, width
    )
    block = lax.all_to_all(pair_elements, "col", split_axis=2, concat_axis=1, tiled=True)
    real_part = jnp.sum(screened[0] * block[0] + screened[1] * block[1], axis=-1)
    imag_part = jnp.sum(screened[0] * block[1] - screened[1] * block[0], axis=-1)
    real_total, imag_total = lax.psum((real_part, imag_part), "col")
    weight = 1.0 / (1.0 + 0.25 * freq_index[0].astype(jnp.float32))
    factor = weight * (0.5 - occupied.astype(jnp.float32)) * NG ** (-0.5)
    sigma_bands = jnp.stack([real_total * factor, imag_total * factor])
    return (screened, sigma_bands)


def solution(mesh):
    placed = (P(None, ("row", "col"), None), P("row", "col"), P("row"), P())
    return jax.shard_map(
        per_device,
        mesh=mesh,
        in_specs=placed,
        out_specs=(P(None, "row", "col"), P(None, "row")),
        check_vma=False,
    )
```

profile of v0, /device:TPU:0, one launch (start us, length us, event | category | flops | bytes accessed | tf_op | source)
XLA Modules:
  0.0 786.5 jit_solution(2600636117080966903)
XLA Ops:
  7.2 0.0 all-gather.2.cloned.1.call-start
  7.2 3.4 copy.12
  10.6 0.0 all-gather.2.cloned.1.call-update
  10.6 0.0 all-reduce.4.cloned.1.call-start
  10.7 128.9 %all-gather.2.cloned.1.call-done = f32[2,64,20480]{2,0,1:T(2,128)} async-done(((f32[2,8,20480]{2,0,1:T(2,128)}), f32[2,64,20480]{2,0,1:T(2,128)}) %all-gather.2.cloned.1.call-update) | async-done | bytes 10485776 | tf_op jit(solution)/shard_map/all_gather | solution.py:23
  139.6 28.5 %copy.13 = f32[2,64,20480]{1,0,2:T(2,128)} copy(f32[2,64,20480]{2,0,1:T(2,128)} %all-gather.2.cloned.1.call-done) | data formatting | bytes 20971520 | tf_op jit(solution)/shard_map/all_gather | solution.py:23
  168.0 25.6 %reshape.30 = f32[16,1,163840]{2,1,0:T(1,128)} reshape(f32[20480,2,64]{2,1,0:T(2,128)} %bitcast.55) | data formatting | bytes 20971520
  193.6 122.6 %all_to_all.30 = f32[16,1,163840]{2,1,0:T(1,128)} all-to-all(f32[16,1,163840]{2,1,0:T(1,128)} %reshape.30), channel_id=1, replica_groups=mesh['row'=16,'col'=8] {'row'}, dimensions={0} | all-to-all | bytes 20971520 | tf_op jit(solution)/shard_map/all_to_all | solution.py:25
  316.3 0.5 broadcast
  316.8 31.0 %reduce = f32[16,163840]{1,0:T(8,128)} reduce(f32[16,1,163840]{2,1,0:T(1,128)} %all_to_all.30, f32[]{:T(128)} %broadcast), dimensions={1}, to_apply=%all_to_all.22.reduce_sub_computation | reduce | bytes 20971524 | tf_op jit(solution)/shard_map/all_to_all | solution.py:25
  347.7 34.2 %reshape.31 = f32[20480,2,64]{2,1,0:T(2,128)} reshape(f32[16,163840]{1,0:T(8,128)} %reduce) | data formatting | bytes 20971520
  381.9 25.0 %copy.15 = f32[2,64,16,1280]{3,1,2,0:T(8,128)} copy(f32[2,64,16,1280]{1,0,3,2:T(2,128)} %bitcast.56) | data formatting | bytes 20971520 | tf_op jit(solution)/shard_map/all_to_all | solution.py:25
  407.0 93.9 %fusion = f32[2,16,64,2560]{3,2,1,0:T(8,128)} fusion(f32[1280,2560]{1,0:T(8,128)} %param.5, f32[2,64,16,1280]{3,1,2,0:T(8,128)} %copy.15), kind=kOutput, calls=%fused_computation | convolution fusion | flops 80530636800 | bytes 44564480 | tf_op jit(solution)/shard_map/kbg,gh->kbh/dot_general | solution.py:10
  500.9 0.0 copy-start
  500.9 0.0 all-reduce.4.cloned.1.call-update
  500.9 1.3 copy-done
  502.2 17.8 %copy.16 = f32[2,8,20480]{1,0,2:T(2,128)} copy(f32[2,8,20480]{2,1,0:T(8,128)S(1)} %copy-done) | data formatting | bytes 2621440 | tf_op args[0]
  520.0 0.0 copy-start.2
  520.0 36.4 %reshape.32 = f32[8,1,40960]{2,1,0:T(1,128)} reshape(f32[20480,2,8]{2,1,0:T(2,128)} %bitcast.54) | data formatting | bytes 2621440
  556.4 4.1 all-to-all-start.1
  561.2 0.0 copy-done.2
  561.3 0.6 dynamic-slice
  561.9 26.1 %all-to-all-done.1 = f32[8,1,40960]{2,1,0:T(1,128)S(1)} async-done(((f32[8,1,40960]{2,1,0:T(1,128)}), f32[8,1,40960]{2,1,0:T(1,128)S(1)}, u32[]{:S(2)}, u32[]{:S(2)}) %all-to-all-start.1) | async-done | bytes 1310752 | tf_op jit(solution)/shard_map/all_to_all | solution.py:32
  588.0 3.8 reduce.1
  591.8 40.2 %reshape.33 = f32[20480,2,8]{2,1,0:T(2,128)} reshape(f32[8,40960]{1,0:T(8,128)S(1)} %reduce.1) | data formatting | bytes 2621440
  632.0 22.0 %copy.17 = f32[2,8,8,2560]{3,1,2,0:T(8,128)S(1)} copy(f32[2,8,8,2560]{1,0,3,2:T(2,128)} %bitcast.53) | data formatting | bytes 2621440 | tf_op jit(solution)/shard_map/all_to_all | solution.py:32
  653.9 95.5 %all-reduce.4.cloned.1.call-done = f32[2,16,64,2560]{3,2,1,0:T(8,128)} async-done(((f32[2,16,64,2560]{3,2,1,0:T(8,128)}), f32[2,16,64,2560]{3,2,1,0:T(8,128)}) %all-reduce.4.cloned.1.call-update) | async-done | bytes 20971536
  749.4 2.2 add_reduce_fusion
  751.6 24.1 %all-reduce.1 = (f32[64]{0:T(128)S(1)}, f32[64]{0:T(128)S(1)}) all-reduce(f32[64]{0:T(128)S(1)} %get-tuple-element.3, f32[64]{0:T(128)S(1)} %get-tuple-element.2), channel_id=1, replica_groups=mesh['row'=16,'col'=8] {'col'}, use_global_device_ids=true, to_apply=%region_4.0 | all-reduce | flops 128 | bytes 1024 | tf_op jit(solution)/shard_map/psum | solution.py:35
  775.7 0.0 copy-done.1
  775.7 0.6 pad_maximum_fusion
  776.3 3.1 dynamic-slice_bitcast_fusion
  (2 shorter events, 0.0 us)
Async XLA Ops:
  7.2 132.4 %all-gather.2.cloned.1.call-start = ((), (), s32[]{:S(2)}) async-start(), calls=%async_computation.2 | async-start | bytes 11796480 | tf_op jit(solution)/shard_map/all_gather | solution.py:23
  10.6 738.8 %all-reduce.4.cloned.1.call-start = ((), (), s32[]{:S(2)}) async-start(), calls=%async_computation.3 | async-start | bytes 41943040
  500.9 1.3 copy-start
  520.0 41.2 %copy-start.2 = (u32[128]{0:T(128)S(1)}, u32[128]{0:T(128)}, u32[]{:S(2)}) copy-start(u32[128]{0:T(128)} %constant.16) | copy-start | bytes 1540
  556.4 31.6 %all-to-all-start.1 = ((f32[8,1,40960]{2,1,0:T(1,128)}), f32[8,1,40960]{2,1,0:T(1,128)S(1)}, u32[]{:S(2)}, u32[]{:S(2)}) async-start(f32[8,1,40960]{2,1,0:T(1,128)} %reshape.32), calls=%async_computation.1 | async-start | bytes 2621440 | tf_op jit(solution)/shard_map/all_to_all | solution.py:32
  631.9 143.8 %copy-start.1 = (s32[64]{0:T(128)S(1)}, s32[64]{0:T(128)}, u32[]{:S(2)}) copy-start(s32[64]{0:T(128)} %param.6) | copy-start | bytes 772
Sparse Core Ops, SparseCore 0:
  10.9 128.6 all-gather.1
  501.1 248.3 all-reduce.3
where the time goes:
time: 792 us; the launch traced here: 786 us
  waiting for transfers between devices  251 us (32%)
  local copies, waits for them, and re-layouts  239 us (30%)
  blocking collectives  147 us (19%)
  matrix products  93.9 us (12%)
  other arithmetic  37.5 us (5%)
  between operations  15 us (2%)
    unnamed x13, local copies, waits for them, and re-layouts  159 us
    all_gather x1, waiting for transfers between devices, per_device(): gathered = lax.all_gather(pair_elements, 'col', axis=1, tiled=True)  129 us
    all_to_all x1, blocking collectives, per_device(): lax.all_to_all(gathered, 'row', split_axis=2, concat_axis=1, tiled=True)  123 us
    unnamed x3, waiting for transfers between devices  95.6 us
    dot_general x1, matrix products, apply_screen(): jnp.einsum('kbg,gh->kbh', block, tile, precision=lax.Precision.HIGHEST, p...  93.9 us
    all_to_all x1, other arithmetic, per_device(): lax.all_to_all(gathered, 'row', split_axis=2, concat_axis=1, tiled=True)  31 us
    all_gather x1, local copies, waits for them, and re-layouts, per_device(): gathered = lax.all_gather(pair_elements, 'col', axis=1, tiled=True)  28.5 us
    all_to_all x1, waiting for transfers between devices, per_device(): lax.all_to_all(pair_elements, 'col', split_axis=2, concat_axis=1, tiled=T...  26.1 us
  transfers between devices with their start and end apart: 3, of which 3 were waited for; matrix products, arithmetic and copies ran while one was open for 15% of the time, Pallas kernels for 0%

commit v1 on v0

v1 whole, which is shorter than its diff:
```python
import functools

import jax
import jax.numpy as jnp
from jax import lax
from jax.experimental import pallas as pl
from jax.experimental.pallas import tpu as pltpu
from jax.sharding import Mesh, PartitionSpec as P

NG = 20480
ROWS = 16
CHIP = 2560
HALF = 1280
TILE = 512
F32 = jnp.float32
BF16 = jnp.bfloat16
SIZES = {"xl": 2, "y": 4, "core": 2, "z": 4, "xh": 2}

OWNERS = ((0, 2), (1, 1), (1, 2), (0, 3), (0, 1), (1, 3), (0, 0), (1, 0))
WAVES = (((0, 0),), ((0, 1), (1, 0), (3, 0)), ((1, 1), (3, 1), (2, 0)), ((2, 1),))


def array(shape, dtype=F32):
    return jax.ShapeDtypeStruct(shape, dtype)


TOKEN = array((8, 128))
KEPT = pl.BlockSpec(memory_space=pltpu.HBM)
ANYWHERE = pl.BlockSpec(memory_space=pl.ANY)


def call(kernel, token, args, outs, in_specs, out_specs, grid, place=None, scratch=(), aliases=None, vmem=8):
    lead = 0 if place is None else 1
    n_in = lead + len(args)

    def body(*refs):
        rest = refs[n_in + 1 :]
        kernel(*refs[:n_in], *rest[: len(outs)], *rest[len(outs) + 1 :])

    result = pl.pallas_call(
        body,
        grid_spec=pltpu.PrefetchScalarGridSpec(
            num_scalar_prefetch=lead,
            grid=grid,
            in_specs=[*in_specs, ANYWHERE],
            out_specs=[*out_specs, ANYWHERE],
            scratch_shapes=list(scratch),
        ),
        out_shape=[*outs, TOKEN],
        input_output_aliases=aliases or {},
        compiler_params=pltpu.CompilerParams(vmem_limit_bytes=vmem << 20),
        cost_estimate=pl.CostEstimate(flops=1024, bytes_accessed=4096, transcendentals=0),
    )(*(() if place is None else (place,)), *args, token)
    return result[:-1], result[-1]


def tie(values, token):
    result = pl.pallas_call(
        lambda *refs: None,
        out_shape=[*(array(v.shape) for v in values), TOKEN],
        in_specs=[KEPT] * len(values) + [ANYWHERE],
        out_specs=[KEPT] * len(values) + [ANYWHERE],
        input_output_aliases={i: i for i in range(len(values))},
        cost_estimate=pl.CostEstimate(flops=1024, bytes_accessed=4096, transcendentals=0),
    )(*values, token)
    return result[:-1], result[-1]


def cut_kernel(place_ref, x_ref, by_row_ref, by_col_ref):
    core = place_ref[0]
    for i in range(8):
        start = pl.multiple_of(i * CHIP + core * HALF, HALF)
        by_row_ref[i, :, :HALF] = x_ref[:, pl.ds(start, HALF)]
        start = pl.multiple_of(i * CHIP + (1 - core) * HALF, HALF)
        by_row_ref[i, :, HALF:] = x_ref[:, pl.ds(start, HALF)]
        by_col_ref[i] = x_ref[:, i * CHIP : (i + 1) * CHIP]


def split(value):
    high = value.astype(BF16)
    return high, (value - high.astype(F32)).astype(BF16)


def halve(w, token):
    def kernel(w_ref, high_ref, low_ref):
        high_ref[0], low_ref[0] = split(w_ref[...])

    return call(
        kernel,
        token,
        [w],
        [array((CHIP // TILE, HALF, TILE), BF16)] * 2,
        [pl.BlockSpec((HALF, TILE), lambda i, *_: (0, i))],
        [pl.BlockSpec((1, HALF, TILE), lambda i, *_: (i, 0, 0))] * 2,
        (CHIP // TILE,),
        vmem=56,
    )


def screen_kernel(first, spare, sizes, place_ref, *refs):
    n_x = sum(sizes)
    x_refs, w_refs = refs[:n_x], refs[n_x : n_x + 3 + (not first)]
    up, down, left, *made, both_ref = refs[n_x + 3 + (not first) :]
    rows, n = 128 * len(sizes), ROWS * len(sizes)

    @pl.when(pl.program_id(0) == 0)
    def _():
        taken = 0
        for i, size in enumerate(sizes):
            for k in range(8):
                parts = [x_ref[place_ref[k]] for x_ref in x_refs[taken : taken + size]]
                high, low = split(parts[0] if size == 1 else jnp.concatenate(parts, axis=0))
                at = i * 128 + k * ROWS
                both_ref[at : at + ROWS, :] = high
                both_ref[rows + at : rows + at + ROWS, :] = low
            taken += size

    own_high, own_low, *other = w_refs
    if first:
        made[0][0], made[1][0] = split(other[0][...])
        other = made
    total = None
    for part, (high, low) in enumerate(((own_high, own_low), other)):
        at = slice(part * HALF, (part + 1) * HALF)
        product = jnp.dot(both_ref[:, at], high[0], preferred_element_type=F32)
        product = product[:rows] + product[rows:]
        product += jnp.dot(both_ref[:rows, at], low[0], preferred_element_type=F32)
        total = product if total is None else total + product
    for i in range(len(sizes)):
        for k, (ref, group) in enumerate(
            ((up, 0), (up, 1), (down, 0), (down, 1), (left, 0), (left, 1), (left, 2), (left, 3))
        ):
            at = (group + spare * (ref is not left)) * n + i * ROWS
            ref[at : at + ROWS, :] = total[i * 128 + k * ROWS : i * 128 + (k + 1) * ROWS]


def screen(owners, chunks, weights, token, spare=0):
    sizes = [len(c) for c in chunks]
    arrays = [a for c in chunks for a in c]
    n = ROWS * len(chunks)
    first = len(weights) == 3
    half = pl.BlockSpec((1, HALF, TILE), lambda i, *_: (i, 0, 0))
    return call(
        functools.partial(screen_kernel, first, spare, sizes),
        token,
        [*arrays, *weights],
        [array((k * n, CHIP)) for k in (2 + spare, 2 + spare, 4)] + [array((CHIP // TILE, HALF, TILE), BF16)] * (2 * first),
        [pl.BlockSpec(a.shape, lambda i, *_: (0, 0, 0)) for a in arrays]
        + [half] * 2
        + ([pl.BlockSpec((HALF, TILE), lambda i, *_: (0, i))] if first else [half] * 2),
        [pl.BlockSpec((k * n, TILE), lambda i, *_: (0, i)) for k in (2 + spare, 2 + spare, 4)] + [half] * (2 * first),
        (CHIP // TILE,),
        place=owners,
        scratch=[pltpu.VMEM((16 * n, CHIP), BF16)],
        vmem=56,
    )


def rows_at(n, *groups):
    tile = CHIP if n <= 16 else CHIP // 2
    return tile, [pl.BlockSpec((k * n, tile), lambda i, *_, at=at: (at, i)) for k, at in groups]


def pass_on(left, up, down, token, spare=0, into=()):
    n = left.shape[0] // 4

    def kernel(left, up, down, *rest):
        to_up, to_down = rest[-2:]
        to_up[...] = left[:n, :] + up[...]
        to_down[...] = left[n:, :] + down[...]

    tile, specs = rows_at(n, (2, 0), (1, spare), (1, spare), (1, 0), (1, 0))
    return call(
        kernel,
        token,
        [left, up, down, *into],
        [array((into[0] if into else up).shape) if into else array((n, CHIP))] * 2,
        specs[:3] + [KEPT] * len(into),
        specs[3:],
        (CHIP // tile,),
        aliases={3: 0, 4: 1} if into else {},
    )


def turn(left, up, down, below, above, token, spare=0):
    n = left.shape[0] // 4
    tile, specs = rows_at(n, (1, 2), (1, 3), (1, 1 + spare), (1, 1 + spare), (1, 0), (1, 0), (1, 0), (1, 0))

    def kernel(stay, go, up, down, below, above, kept, out):
        out[...] = go[...] + up[...] + above[...]
        kept[...] = stay[...] + down[...] + below[...]

    return call(
        kernel,
        token,
        [left, left, up, down, below, above],
        [array((n, CHIP))] * 2,
        specs[:6],
        specs[6:],
        (CHIP // tile,),
    )


def finish(place, kept, across, block, held, token):
    def kernel(place_ref, kept, across, block, *rest):
        out, sums = rest[-2:]
        value = kept[...] + across[...]
        out[0] = value[:8]
        out[1] = value[8:]
        real, imag = block[0, :8, :], block[0, 8:, :]
        sums[0, :8, :] = jnp.sum(value[:8] * real + value[8:] * imag, axis=-1, keepdims=True)
        sums[0, 8:, :] = jnp.sum(value[:8] * imag - value[8:] * real, axis=-1, keepdims=True)

    return call(
        kernel,
        token,
        [kept, across, block, *held],
        [array((2, 64, CHIP)), array((8, ROWS, 1))],
        [pl.BlockSpec((ROWS, CHIP), lambda i, p, k=k: (k + i, 0)) for k in (0, 0)]
        + [pl.BlockSpec((1, ROWS, CHIP), lambda i, p: (p[i], 0, 0))]
        + [KEPT] * len(held),
        [
            pl.BlockSpec((2, 8, CHIP), lambda i, p: (0, p[i], 0)),
            pl.BlockSpec((1, ROWS, 1), lambda i, p: (p[i], 0, 0)),
        ],
        (kept.shape[0] // ROWS,),
        place=place,
        aliases={4: 0, 5: 1} if held else {},
    )


def move(value, axis, by):
    size = SIZES[axis]
    return lax.ppermute(value, axis, [(i, (i + by) % size) for i in range(size)])


def per_device(pair_elements, screened_w, occupied, freq_index):
    xl, y, core, z, xh = [lax.axis_index(a) for a in SIZES]
    other = move(screened_w, "core", 1)
    owners = jnp.stack([(xl + a) % 2 * 4 + (y + b) % 4 for a, b in OWNERS]).astype(jnp.int32)
    places = jnp.stack([(z + a) % 4 * 2 + (xh + b) % 2 for w in WAVES for a, b in w]).astype(jnp.int32)
    weight = 1.0 / (1.0 + 0.25 * freq_index[0].astype(F32))
    factor = weight * (0.5 - occupied.astype(F32)) * NG ** (-0.5)

    token = jnp.zeros((8, 128), F32)
    whole3 = pl.BlockSpec((8, ROWS, CHIP), lambda i, *_: (0, 0, 0))
    (by_row, by_col), token = call(
        cut_kernel,
        token,
        [pair_elements.reshape(ROWS, NG)],
        [array((8, ROWS, CHIP))] * 2,
        [pl.BlockSpec((ROWS, NG), lambda i, *_: (0, 0))],
        [whole3] * 2,
        (1,),
        vmem=12,
        place=core.astype(jnp.int32).reshape(1),
    )
    with jax.named_scope("rows_to_their_plane_waves"):
        mine = lax.all_to_all(by_row, ("xl", "y"), 0, 0, tiled=True)
    halves, token = halve(screened_w, token)
    (mine,), token = tie([mine], token)
    chunk = {(0, 0): mine}
    with jax.named_scope("near_chunks"):
        chunk[0, 1] = move(mine, "xh", 1)
        chunk[3, 0] = move(mine, "z", 1)
        chunk[1, 0] = move(mine, "z", -1)

    (up0, down0, left0, *more), token = screen(owners, [[mine]], [*halves, other], token)
    halves = [*halves, *more]
    up0, down0 = move(up0, "y", 1), move(down0, "y", -1)
    (to_up, to_down), token = pass_on(left0, up0, down0, token)
    below0, above0 = move(to_up, "y", 1), move(to_down, "y", -1)

    with jax.named_scope("far_chunks"):
        got, token = tie([chunk[c] for c in WAVES[1]], token)
        chunk |= dict(zip(WAVES[1], got))
        chunk[1, 1] = move(chunk[1, 0], "xh", 1)
        chunk[3, 1] = move(chunk[0, 1], "z", 1)
        chunk[2, 0] = move(chunk[1, 0], "z", -1)

    (up1, down1, left1), token = screen(owners, [[chunk[c]] for c in WAVES[1]], halves, token)
    up1, down1 = move(up1, "y", 1), move(down1, "y", -1)
    (kept0, across0), token = turn(left0, up0, down0, below0, above0, token)
    across0 = move(across0, "xl", 1)

    with jax.named_scope("last_chunk"):
        got, token = tie([chunk[c] for c in WAVES[2]], token)
        chunk |= dict(zip(WAVES[2], got))
        last = [move(chunk[3, 1][:, :8], "z", 1), move(chunk[1, 1][:, 8:], "z", -1)]

    (up2, down2, left2), token = screen(owners, [[chunk[c]] for c in WAVES[2]], halves, token, 1)
    (up2, down2), token = pass_on(left1, up1, down1, token, 0, (up2, down2))
    up2, down2 = move(up2, "y", 1), move(down2, "y", -1)
    (*last, by_col), token = tie([*last, by_col], token)
    with jax.named_scope("second_index"):
        block = lax.all_to_all(by_col, ("z", "xh"), 0, 0, tiled=True)

    (up3, down3, left3), token = screen(owners, [last], halves, token)
    up3, down3 = move(up3, "y", 1), move(down3, "y", -1)

    held, token = finish(places[:1], kept0, across0, block, (), token)
    (to_up, to_down), token = pass_on(left2, up2, down2, token, 1)
    below2, above2 = move(to_up, "y", 1), move(to_down, "y", -1)
    (kept1, across1), token = turn(left1, up1, down1, up2, down2, token)
    across1 = move(across1, "xl", 1)
    (to_up, to_down), token = pass_on(left3, up3, down3, token)
    below3, above3 = move(to_up, "y", 1), move(to_down, "y", -1)
    (kept2, across2), token = turn(left2, up2, down2, below2, above2, token, 1)
    across2 = move(across2, "xl", 1)
    (kept3, across3), token = turn(left3, up3, down3, below3, above3, token)
    across3 = move(across3, "xl", 1)
    held, token = finish(places[1:4], kept1, across1, block, held, token)
    held, token = finish(places[4:7], kept2, across2, block, held, token)
    (out, sums), token = finish(places[7:], kept3, across3, block, held, token)

    with jax.named_scope("bands"):
        sums = sums.reshape(8, 2, 8).transpose(1, 0, 2).reshape(2, 64)
        sums = sums + move(sums, "xh", 1)
        for pairs in ([1, 0, 3, 2], [2, 3, 0, 1]):
            sums = sums + lax.ppermute(sums, "z", list(enumerate(pairs)))
    return out, sums * factor


def solution(mesh):
    fine = Mesh(mesh.devices.reshape(2, 4, 2, 4, 2), tuple(SIZES))
    row, col = ("xl", "y", "core"), ("z", "xh")
    return jax.shard_map(
        per_device,
        mesh=fine,
        in_specs=(P(None, row + col, None), P(row, col), P(row), P()),
        out_specs=(P(None, row, col), P(None, row)),
        check_vma=False,
    )
```

time: 792 us -> 223 us (0.28)
  local copies, waits for them, and re-layouts: 239 us -> 18.1 us
  waiting for transfers between devices: 251 us -> 40.9 us
  blocking collectives: 147 us -> 0 us
  Pallas kernels: 0 us -> 107 us
  matrix products: 93.9 us -> 0 us
  starting transfers between devices: 4.23 us -> 53.5 us
  other arithmetic: 37.5 us -> 0.82 us
  between operations: 15 us -> 1.58 us
    unnamed x13 -> x74, local copies, waits for them, and re-layouts: 159 us -> 16.1 us
    all_gather x1 -> x0, waiting for transfers between devices: 129 us -> none  [per_device(): gathered = lax.all_gather(pair_elements, 'col', axis=1, tiled=True)]
    all_to_all x1 -> x0, blocking collectives: 123 us -> none  [per_device(): lax.all_to_all(gathered, 'row', split_axis=2, concat_axis=1, tiled=True)]
    pallas_call x0 -> x22, Pallas kernels: none -> 107 us  [the longest x18 107 us: call(): pl.pallas_call(body, grid_spec=pltpu.PrefetchScalarGridSpec(num_scalar_pr...]
    unnamed x3 -> x0, waiting for transfers between devices: 95.6 us -> none
    dot_general x1 -> x0, matrix products: 93.9 us -> none  [apply_screen(): jnp.einsum('kbg,gh->kbh', block, tile, precision=lax.Precision.HIGHEST, p...]
    all_to_all x3 -> x0, local copies, waits for them, and re-layouts: 47.5 us -> none  [the longest x2 25.6 us: per_device(): lax.all_to_all(gathered, 'row', split_axis=2, concat_axis=1, tiled=True)]
    ppermute x0 -> x30, starting transfers between devices: none -> 44 us  [the longest x28 43.8 us: move(): lax.ppermute(value, axis, [(i, (i + by) % size) for i in range(size)])]
  transfers between devices with their start and end apart: 3 -> 32, of which waited for: 3 -> 11; matrix products, arithmetic and copies ran while one was open for 15% -> 1% of each run, Pallas kernels for 0% -> 47%
where the time goes in v1:
time: 223 us; the launch traced here: 222 us
  Pallas kernels  107 us (48%)
  starting transfers between devices  53.5 us (24%)
  waiting for transfers between devices  40.9 us (18%)
  local copies, waits for them, and re-layouts  18.1 us (8%)
    pallas_call x18, Pallas kernels, call(): pl.pallas_call(body, grid_spec=pltpu.PrefetchScalarGridSpec(num_scalar_pr...  107 us
    ppermute x28, starting transfers between devices, move(): lax.ppermute(value, axis, [(i, (i + by) % size) for i in range(size)])  43.8 us
    ppermute x28, waiting for transfers between devices, move(): lax.ppermute(value, axis, [(i, (i + by) % size) for i in range(size)])  24.1 us
    unnamed x74, local copies, waits for them, and re-layouts  16.1 us
    ppermute x2, waiting for transfers between devices, per_device(): sums = sums + lax.ppermute(sums, 'z', list(enumerate(pairs)))  7.71 us
    all_to_all x1, waiting for transfers between devices, per_device(): mine = lax.all_to_all(by_row, ('xl', 'y'), 0, 0, tiled=True)  6.88 us
    all_to_all x1, starting transfers between devices, per_device(): mine = lax.all_to_all(by_row, ('xl', 'y'), 0, 0, tiled=True)  5.48 us
  transfers between devices with their start and end apart: 32, of which 11 were waited for; matrix products, arithmetic and copies ran while one was open for 1% of the time, Pallas kernels for 47%

profile of v1, /device:TPU:0, one launch (start us, length us, event | category | flops | bytes accessed | tf_op | source)
XLA Modules:
  0.0 222.3 jit_solution(2073920694723072398)
XLA Ops:
  5.0 5.5 %all-to-all-start = ((f32[8,16,2560]{2,1,0:T(8,128)}), f32[8,16,2560]{2,1,0:T(8,128)S(1)}, u32[]{:S(2)}, u32[]{:S(2)}) async-start(f32[8,16,2560]{2,1,0:T(8,128)} %get-tuple-element.75), calls=%async_computation | async-start | bytes 2621440 | tf_op jit(solution)/shard_map/rows_to_their_plane_waves/all_to_all | solution.py:259
  10.4 11.4 %shard_map.60 = (bf16[5,1280,512]{2,1,0:T(8,128)(2,1)}, bf16[5,1280,512]{2,1,0:T(8,128)(2,1)}, f32[8,128]{1,0:T(8,128)}) custom-call(f32[1280,2560]{1,0:T(8,128)} %refs_0_.1, f32[8,128]{1,0:T(8,128)} %copy-done.28), custom_call_target="tpu_custom_call" | custom-call | flops 1024 | bytes 4096 | tf_op jit(solution)/shard_map/pallas_call | solution.py:40
  21.8 6.9 %all-to-all-done.refs_0_ = f32[8,16,2560]{2,1,0:T(8,128)S(1)} async-done(((f32[8,16,2560]{2,1,0:T(8,128)}), f32[8,16,2560]{2,1,0:T(8,128)S(1)}, u32[]{:S(2)}, u32[]{:S(2)}) %all-to-all-start) | async-done | bytes 1310752 | tf_op jit(solution)/shard_map/rows_to_their_plane_waves/all_to_all | solution.py:259
  29.7 2.7 %collective-permute-start = (f32[8,16,2560]{2,1,0:T(8,128)}, f32[8,16,2560]{2,1,0:T(8,128)}, u32[]{:S(2)}, u32[]{:S(2)}) collective-permute-start(f32[8,16,2560]{2,1,0:T(8,128)} %get-tuple-element.78.refs_1_), channel_id=1, source_target_pairs={{0,1},{1,0},{2,3},{3,2},{4,5},{5,4},{6,7},{7,6},{8,9},{9,8},{10,11... | collective-permute-start | bytes 3932168 | tf_op jit(solution)/shard_map/near_chunks/ppermute | solution.py:234
  32.5 4.0 %collective-permute-start.1 = (f32[8,16,2560]{2,1,0:T(8,128)}, f32[8,16,2560]{2,1,0:T(8,128)}, u32[]{:S(2)}, u32[]{:S(2)}) collective-permute-start(f32[8,16,2560]{2,1,0:T(8,128)} %get-tuple-element.78.refs_1_), channel_id=1, source_target_pairs={{0,6},{2,0},{4,2},{6,4},{1,7},{3,1},{5,3},{7,5},{8,14},{10,8},{12,... | collective-permute-start | bytes 3932168 | tf_op jit(solution)/shard_map/near_chunks/ppermute | solution.py:234
  37.2 17.4 %shard_map.62 = (f32[32,2560]{1,0:T(8,128)}, f32[32,2560]{1,0:T(8,128)}, f32[64,2560]{1,0:T(8,128)}, bf16[5,1280,512]{2,1,0:T(8,128)(2,1)}, bf16[5,1280,512]{2,1,0:T(8,128)(2,1)}, /*index=5*/f32[8,128]{1,0:T(8,128)}) custom-call(s32[8]{0:T(128)} %stack.65.refs_0_, f32[8,16,2560]{2,1,0:T(8,128)} %get-tuple-element.78.refs_1_, ...), custom_call_target="tpu_custom_call" | custom-call | flops 1024 | bytes 4096 | tf_op jit(solution)/shard_map/pallas_call | solution.py:40
  55.5 2.4 %collective-permute-start.5 = (f32[32,2560]{1,0:T(8,128)}, f32[32,2560]{1,0:T(8,128)S(1)}, u32[]{:S(2)}, u32[]{:S(2)}) collective-permute-start(f32[32,2560]{1,0:T(8,128)} %get-tuple-element.84), channel_id=1, source_target_pairs={{0,48},{16,0},{32,16},{48,32},{1,49},{17,1},{33,17},{49,33},{2,50}... | collective-permute-start | bytes 983048 | tf_op jit(solution)/shard_map/ppermute | solution.py:234
  57.9 7.0 %collective-permute-done.4.refs_1_.refs_2_ = f32[32,2560]{1,0:T(8,128)S(1)} collective-permute-done((f32[32,2560]{1,0:T(8,128)}, f32[32,2560]{1,0:T(8,128)S(1)}, u32[]{:S(2)}, u32[]{:S(2)}) %collective-permute-start.4) | collective-permute-done | bytes 327712 | tf_op jit(solution)/shard_map/ppermute | solution.py:234
  69.7 3.2 %collective-permute-start.8 = (f32[8,16,2560]{2,1,0:T(8,128)}, f32[8,16,2560]{2,1,0:T(8,128)}, u32[]{:S(2)}, u32[]{:S(2)}) collective-permute-start(f32[8,16,2560]{2,1,0:T(8,128)} %get-tuple-element.87.refs_2_), channel_id=1, source_target_pairs={{0,6},{2,0},{4,2},{6,4},{1,7},{3,1},{5,3},{7,5},{8,14},{10,8},{12,... | collective-permute-start | bytes 3932168 | tf_op jit(solution)/shard_map/far_chunks/ppermute | solution.py:234
  72.9 2.4 %collective-permute-start.10 = (f32[16,2560]{1,0:T(8,128)S(1)}, f32[16,2560]{1,0:T(8,128)S(1)}, u32[]{:S(2)}, u32[]{:S(2)}) collective-permute-start(f32[16,2560]{1,0:T(8,128)S(1)} %get-tuple-element.90), channel_id=1, source_target_pairs={{0,48},{16,0},{32,16},{48,32},{1,49},{17,1},{33,17},{49,33},{2,50}... | collective-permute-start | bytes 491528 | tf_op jit(solution)/shard_map/ppermute | solution.py:234
  75.4 22.4 %shard_map.64 = (f32[96,2560]{1,0:T(8,128)}, f32[96,2560]{1,0:T(8,128)}, f32[192,2560]{1,0:T(8,128)}, f32[8,128]{1,0:T(8,128)}) custom-call(s32[8]{0:T(128)} %stack.65.refs_0_, f32[8,16,2560]{2,1,0:T(8,128)} %get-tuple-element.88.refs_1_, f32[8,16,2560]{2,1,0:T(8,128)} %get-tuple-element.87.refs_2_, f32[8,16,2560]{2,1,0:T(8,128)} %get-tuple-element.91.refs_3_, ...), custom_call_target="tpu_custom_call" | custom-call | flops 1024 | bytes 4096 | tf_op jit(solution)/shard_map/pallas_call | solution.py:40
  97.9 3.3 %collective-permute-start.14 = (f32[96,2560]{1,0:T(8,128)}, f32[96,2560]{1,0:T(8,128)}, u32[]{:S(2)}, u32[]{:S(2)}) collective-permute-start(f32[96,2560]{1,0:T(8,128)} %get-tuple-element.102), channel_id=1, source_target_pairs={{0,48},{16,0},{32,16},{48,32},{1,49},{17,1},{33,17},{49,33},{2,50}... | collective-permute-start | bytes 2949128 | tf_op jit(solution)/shard_map/ppermute | solution.py:234
  105.8 3.3 %collective-permute-start.12 = (f32[8,8,2560]{2,1,0:T(8,128)S(1)}, f32[8,8,2560]{2,1,0:T(8,128)}, u32[]{:S(2)}, u32[]{:S(2)}) collective-permute-start(f32[8,8,2560]{2,1,0:T(8,128)S(1)} %slice.11), channel_id=1, source_target_pairs={{0,6},{2,0},{4,2},{6,4},{1,7},{3,1},{5,3},{7,5},{8,14},{10,8},{12,... | collective-permute-start | bytes 1966088 | tf_op jit(solution)/shard_map/last_chunk/ppermute | solution.py:234
  109.1 22.5 %shard_map.66 = (f32[144,2560]{1,0:T(8,128)}, f32[144,2560]{1,0:T(8,128)}, f32[192,2560]{1,0:T(8,128)}, f32[8,128]{1,0:T(8,128)}) custom-call(s32[8]{0:T(128)} %stack.65.refs_0_, f32[8,16,2560]{2,1,0:T(8,128)} %get-tuple-element.98.refs_1_, f32[8,16,2560]{2,1,0:T(8,128)} %get-tuple-element.97.refs_2_, f32[8,16,2560]{2,1,0:T(8,128)} %get-tuple-element.103.refs_3_, ...), custom_call_target="tpu_custom_call" | custom-call | flops 1024 | bytes 4096 | tf_op jit(solution)/shard_map/pallas_call | solution.py:40
  134.4 3.2 %collective-permute-start.18 = (f32[144,2560]{1,0:T(8,128)}, f32[144,2560]{1,0:T(8,128)}, u32[]{:S(2)}, u32[]{:S(2)}) collective-permute-start(f32[144,2560]{1,0:T(8,128)} %get-tuple-element.116), channel_id=1, source_target_pairs={{0,48},{16,0},{32,16},{48,32},{1,49},{17,1},{33,17},{49,33},{2,50}... | collective-permute-start | bytes 4423688 | tf_op jit(solution)/shard_map/ppermute | solution.py:234
  137.6 4.0 %all-to-all-start.1 = ((f32[8,16,2560]{2,1,0:T(8,128)}), f32[8,16,2560]{2,1,0:T(8,128)S(1)}, u32[]{:S(2)}, u32[]{:S(2)}) async-start(f32[8,16,2560]{2,1,0:T(8,128)} %get-tuple-element.120), calls=%async_computation.1 | async-start | bytes 2621440 | tf_op jit(solution)/shard_map/second_index/all_to_all | solution.py:296
  142.8 13.7 %shard_map.69 = (f32[32,2560]{1,0:T(8,128)}, f32[32,2560]{1,0:T(8,128)}, f32[64,2560]{1,0:T(8,128)}, f32[8,128]{1,0:T(8,128)}) custom-call(s32[8]{0:T(128)} %stack.65.refs_0_, f32[8,8,2560]{2,1,0:T(8,128)} %get-tuple-element.109.refs_1_, f32[8,8,2560]{2,1,0:T(8,128)} %get-tuple-element.110.refs_2_, ...), custom_call_target="tpu_custom_call" | custom-call | flops 1024 | bytes 4096 | tf_op jit(solution)/shard_map/pallas_call | solution.py:40
  156.5 2.2 all-to-all-done.1.refs_3_
  161.1 4.8 %collective-permute-done.17.refs_1_.refs_4_.refs_2_ = f32[144,2560]{1,0:T(8,128)} collective-permute-done((f32[144,2560]{1,0:T(8,128)}, f32[144,2560]{1,0:T(8,128)}, u32[]{:S(2)}, u32[]{:S(2)}) %collective-permute-start.17) | collective-permute-done | bytes 1474592 | tf_op jit(solution)/shard_map/ppermute | solution.py:234
  169.0 3.2 %collective-permute-start.23 = (f32[48,2560]{1,0:T(8,128)S(1)}, f32[48,2560]{1,0:T(8,128)S(1)}, u32[]{:S(2)}, u32[]{:S(2)}) collective-permute-start(f32[48,2560]{1,0:T(8,128)S(1)} %get-tuple-element.128), channel_id=1, source_target_pairs={{0,48},{16,0},{32,16},{48,32},{1,49},{17,1},{33,17},{49,33},{2,50}... | collective-permute-start | bytes 1474568 | tf_op jit(solution)/shard_map/ppermute | solution.py:234
  172.3 3.2 %collective-permute-start.16 = (f32[32,2560]{1,0:T(8,128)S(1)}, f32[32,2560]{1,0:T(8,128)S(1)}, u32[]{:S(2)}, u32[]{:S(2)}) collective-permute-start(f32[32,2560]{1,0:T(8,128)S(1)} %copy-done.34), channel_id=1, source_target_pairs={{0,48},{16,0},{32,16},{48,32},{1,49},{17,1},{33,17},{49,33},{2,50}... | collective-permute-start | bytes 983048 | tf_op jit(solution)/shard_map/ppermute | solution.py:234
  175.5 2.5 %shard_map.72 = (f32[48,2560]{1,0:T(8,128)S(1)}, f32[48,2560]{1,0:T(8,128)}, f32[8,128]{1,0:T(8,128)S(1)}) custom-call(f32[192,2560]{1,0:T(8,128)S(1)} %copy-done, f32[192,2560]{1,0:T(8,128)S(1)} %copy-done, f32[96,2560]{1,0:T(8,128)S(1)} %copy-done.9, f32[96,2560]{1,0:T(8,128)} %collective-permute-done.14.refs_2_.refs_3_, ...), custom_call_target="tpu_custom_call" | custom-call | flops 1024 | bytes 4096 | tf_op jit(solution)/shard_map/pallas_call | solution.py:40
  179.5 5.8 %collective-permute-done.15.refs_1_.refs_2_ = f32[32,2560]{1,0:T(8,128)S(1)} collective-permute-done((f32[32,2560]{1,0:T(8,128)S(1)}, f32[32,2560]{1,0:T(8,128)S(1)}, u32[]{:S(2)}, u32[]{:S(2)}) %collective-permute-start.15) | collective-permute-done | bytes 327712 | tf_op jit(solution)/shard_map/ppermute | solution.py:234
  186.2 2.3 %shard_map.74 = (f32[48,2560]{1,0:T(8,128)S(1)}, f32[48,2560]{1,0:T(8,128)}, f32[8,128]{1,0:T(8,128)S(1)}) custom-call(f32[192,2560]{1,0:T(8,128)S(1)} %copy-done.2, f32[192,2560]{1,0:T(8,128)S(1)} %copy-done.2, f32[144,2560]{1,0:T(8,128)} %collective-permute-done.17.refs_1_.refs_4_.refs_2_, f32[144,2560]{1,0:T(8,128)} %collective-permute-done.18.refs_2_.refs_5_.refs_3_, ...), custom_call_target="tpu_custom_call" | custom-call | flops 1024 | bytes 4096 | tf_op jit(solution)/shard_map/pallas_call | solution.py:40
  191.5 2.4 %collective-permute-start.21 = (f32[16,2560]{1,0:T(8,128)}, f32[16,2560]{1,0:T(8,128)S(1)}, u32[]{:S(2)}, u32[]{:S(2)}) collective-permute-start(f32[16,2560]{1,0:T(8,128)} %get-tuple-element.126), channel_id=1, source_target_pairs={{0,48},{16,0},{32,16},{48,32},{1,49},{17,1},{33,17},{49,33},{2,50}... | collective-permute-start | bytes 491528 | tf_op jit(solution)/shard_map/ppermute | solution.py:234
  194.0 3.5 %collective-permute-done.20.refs_4_ = f32[16,2560]{1,0:T(8,128)S(1)} collective-permute-done((f32[16,2560]{1,0:T(8,128)}, f32[16,2560]{1,0:T(8,128)S(1)}, u32[]{:S(2)}, u32[]{:S(2)}) %collective-permute-start.20) | collective-permute-done | bytes 163872 | tf_op jit(solution)/shard_map/ppermute | solution.py:234
  200.5 3.3 %shard_map.76 = (f32[2,64,2560]{2,1,0:T(8,128)}, f32[8,16,1]{2,1,0:T(8,128)S(1)}, f32[8,128]{1,0:T(8,128)S(1)}) custom-call(s32[3]{0:T(128)S(1)} %pad_add_fusion.1.refs_0_, f32[48,2560]{1,0:T(8,128)S(1)} %copy-done.16, f32[48,2560]{1,0:T(8,128)} %collective-permute-done.26.refs_2_, ...), custom_call_target="tpu_custom_call", output_to_operand_aliasing={{0}: (4, {}), {1}: (5, {})} | custom-call | flops 1024 | bytes 4096 | tf_op jit(solution)/shard_map/pallas_call | solution.py:40
  203.8 3.3 %shard_map.77 = (f32[2,64,2560]{2,1,0:T(8,128)}, f32[8,16,1]{2,1,0:T(8,128)S(1)}, f32[8,128]{1,0:T(8,128)S(1)}) custom-call(s32[3]{0:T(128)S(1)} %pad_add_fusion.refs_0_, f32[48,2560]{1,0:T(8,128)S(1)} %copy-done.18, f32[48,2560]{1,0:T(8,128)} %collective-permute-done.25.refs_2_, ...), custom_call_target="tpu_custom_call", output_to_operand_aliasing={{0}: (4, {}), {1}: (5, {})} | custom-call | flops 1024 | bytes 4096 | tf_op jit(solution)/shard_map/pallas_call | solution.py:40
  208.0 2.7 %collective-permute-start.27 = (f32[2,64]{1,0:T(2,128)S(1)}, f32[2,64]{1,0:T(2,128)S(1)}, u32[]{:S(2)}, u32[]{:S(2)}) collective-permute-start(f32[2,64]{1,0:T(2,128)S(1)} %reshape.27), channel_id=1, source_target_pairs={{0,1},{1,0},{2,3},{3,2},{4,5},{5,4},{6,7},{7,6},{8,9},{9,8},{10,11... | collective-permute-start | bytes 1544 | tf_op jit(solution)/shard_map/bands/ppermute | solution.py:234
  210.7 2.3 %collective-permute-done.27 = f32[2,64]{1,0:T(2,128)S(1)} collective-permute-done((f32[2,64]{1,0:T(2,128)S(1)}, f32[2,64]{1,0:T(2,128)S(1)}, u32[]{:S(2)}, u32[]{:S(2)}) %collective-permute-start.27) | collective-permute-done | bytes 544 | tf_op jit(solution)/shard_map/bands/ppermute | solution.py:234
  213.8 2.9 %collective-permute-done.28 = f32[2,64]{1,0:T(2,128)S(1)} collective-permute-done((f32[2,64]{1,0:T(2,128)S(1)}, f32[2,64]{1,0:T(2,128)S(1)}, u32[]{:S(2)}, u32[]{:S(2)}) %collective-permute-start.28) | collective-permute-done | bytes 544 | tf_op jit(solution)/shard_map/bands/ppermute | solution.py:320
  216.9 4.8 %collective-permute-done.29 = f32[2,64]{1,0:T(2,128)S(1)} collective-permute-done((f32[2,64]{1,0:T(2,128)S(1)}, f32[2,64]{1,0:T(2,128)S(1)}, u32[]{:S(2)}, u32[]{:S(2)}) %collective-permute-start.29) | collective-permute-done | bytes 544 | tf_op jit(solution)/shard_map/bands/ppermute | solution.py:320
  (142 shorter events, 36.2 us)
Async XLA Ops:
  0.6 36.5 %collective-permute-start.3 = (f32[1280,2560]{1,0:T(8,128)}, f32[1280,2560]{1,0:T(8,128)}, u32[]{:S(2)}, u32[]{:S(2)}) collective-permute-start(f32[1280,2560]{1,0:T(8,128)} %refs_0_.1), channel_id=1, source_target_pairs={{0,8},{8,0},{1,9},{9,1},{2,10},{10,2},{3,11},{11,3},{4,12},{12,4},... | collective-permute-start | bytes 39321608 | tf_op jit(solution)/shard_map/ppermute | solution.py:234
  5.0 23.7 %all-to-all-start = ((f32[8,16,2560]{2,1,0:T(8,128)}), f32[8,16,2560]{2,1,0:T(8,128)S(1)}, u32[]{:S(2)}, u32[]{:S(2)}) async-start(f32[8,16,2560]{2,1,0:T(8,128)} %get-tuple-element.75), calls=%async_computation | async-start | bytes 2621440 | tf_op jit(solution)/shard_map/rows_to_their_plane_waves/all_to_all | solution.py:259
  29.7 37.5 %collective-permute-start = (f32[8,16,2560]{2,1,0:T(8,128)}, f32[8,16,2560]{2,1,0:T(8,128)}, u32[]{:S(2)}, u32[]{:S(2)}) collective-permute-start(f32[8,16,2560]{2,1,0:T(8,128)} %get-tuple-element.78.refs_1_), channel_id=1, source_target_pairs={{0,1},{1,0},{2,3},{3,2},{4,5},{5,4},{6,7},{7,6},{8,9},{9,8},{10,11... | collective-permute-start | bytes 3932168 | tf_op jit(solution)/shard_map/near_chunks/ppermute | solution.py:234
  32.5 34.8 %collective-permute-start.1 = (f32[8,16,2560]{2,1,0:T(8,128)}, f32[8,16,2560]{2,1,0:T(8,128)}, u32[]{:S(2)}, u32[]{:S(2)}) collective-permute-start(f32[8,16,2560]{2,1,0:T(8,128)} %get-tuple-element.78.refs_1_), channel_id=1, source_target_pairs={{0,6},{2,0},{4,2},{6,4},{1,7},{3,1},{5,3},{7,5},{8,14},{10,8},{12,... | collective-permute-start | bytes 3932168 | tf_op jit(solution)/shard_map/near_chunks/ppermute | solution.py:234
  36.5 31.3 %collective-permute-start.2 = (f32[8,16,2560]{2,1,0:T(8,128)}, f32[8,16,2560]{2,1,0:T(8,128)S(1)}, u32[]{:S(2)}, u32[]{:S(2)}) collective-permute-start(f32[8,16,2560]{2,1,0:T(8,128)} %get-tuple-element.78.refs_1_), channel_id=1, source_target_pairs={{0,2},{2,4},{4,6},{6,0},{1,3},{3,5},{5,7},{7,1},{8,10},{10,12},{12... | collective-permute-start | bytes 3932168 | tf_op jit(solution)/shard_map/near_chunks/ppermute | solution.py:234
  54.6 10.3 %collective-permute-start.4 = (f32[32,2560]{1,0:T(8,128)}, f32[32,2560]{1,0:T(8,128)S(1)}, u32[]{:S(2)}, u32[]{:S(2)}) collective-permute-start(f32[32,2560]{1,0:T(8,128)} %get-tuple-element.83), channel_id=1, source_target_pairs={{0,16},{16,32},{32,48},{48,0},{1,17},{17,33},{33,49},{49,1},{2,18}... | collective-permute-start | bytes 983048 | tf_op jit(solution)/shard_map/ppermute | solution.py:234
  55.5 9.4 %collective-permute-start.5 = (f32[32,2560]{1,0:T(8,128)}, f32[32,2560]{1,0:T(8,128)S(1)}, u32[]{:S(2)}, u32[]{:S(2)}) collective-permute-start(f32[32,2560]{1,0:T(8,128)} %get-tuple-element.84), channel_id=1, source_target_pairs={{0,48},{16,0},{32,16},{48,32},{1,49},{17,1},{33,17},{49,33},{2,50}... | collective-permute-start | bytes 983048 | tf_op jit(solution)/shard_map/ppermute | solution.py:234
  68.9 34.3 %collective-permute-start.6 = (f32[8,16,2560]{2,1,0:T(8,128)}, f32[8,16,2560]{2,1,0:T(8,128)S(1)}, u32[]{:S(2)}, u32[]{:S(2)}) collective-permute-start(f32[8,16,2560]{2,1,0:T(8,128)} %get-tuple-element.87.refs_2_), channel_id=1, source_target_pairs={{0,1},{1,0},{2,3},{3,2},{4,5},{5,4},{6,7},{7,6},{8,9},{9,8},{10,11... | collective-permute-start | bytes 3932168 | tf_op jit(solution)/shard_map/far_chunks/ppermute | solution.py:234
  69.7 33.5 %collective-permute-start.7 = (f32[8,16,2560]{2,1,0:T(8,128)}, f32[8,16,2560]{2,1,0:T(8,128)}, u32[]{:S(2)}, u32[]{:S(2)}) collective-permute-start(f32[8,16,2560]{2,1,0:T(8,128)} %get-tuple-element.88.refs_1_), channel_id=1, source_target_pairs={{0,2},{2,4},{4,6},{6,0},{1,3},{3,5},{5,7},{7,1},{8,10},{10,12},{12... | collective-permute-start | bytes 3932168 | tf_op jit(solution)/shard_map/far_chunks/ppermute | solution.py:234
  69.7 33.5 %collective-permute-start.8 = (f32[8,16,2560]{2,1,0:T(8,128)}, f32[8,16,2560]{2,1,0:T(8,128)}, u32[]{:S(2)}, u32[]{:S(2)}) collective-permute-start(f32[8,16,2560]{2,1,0:T(8,128)} %get-tuple-element.87.refs_2_), channel_id=1, source_target_pairs={{0,6},{2,0},{4,2},{6,4},{1,7},{3,1},{5,3},{7,5},{8,14},{10,8},{12,... | collective-permute-start | bytes 3932168 | tf_op jit(solution)/shard_map/far_chunks/ppermute | solution.py:234
  72.9 24.8 %collective-permute-start.10 = (f32[16,2560]{1,0:T(8,128)S(1)}, f32[16,2560]{1,0:T(8,128)S(1)}, u32[]{:S(2)}, u32[]{:S(2)}) collective-permute-start(f32[16,2560]{1,0:T(8,128)S(1)} %get-tuple-element.90), channel_id=1, source_target_pairs={{0,48},{16,0},{32,16},{48,32},{1,49},{17,1},{33,17},{49,33},{2,50}... | collective-permute-start | bytes 491528 | tf_op jit(solution)/shard_map/ppermute | solution.py:234
  75.4 22.5 %collective-permute-start.9 = (f32[16,2560]{1,0:T(8,128)S(1)}, f32[16,2560]{1,0:T(8,128)S(1)}, u32[]{:S(2)}, u32[]{:S(2)}) collective-permute-start(f32[16,2560]{1,0:T(8,128)S(1)} %get-tuple-element.89), channel_id=1, source_target_pairs={{0,16},{16,32},{32,48},{48,0},{1,17},{17,33},{33,49},{49,1},{2,18}... | collective-permute-start | bytes 491528 | tf_op jit(solution)/shard_map/ppermute | solution.py:234
  97.8 33.8 %collective-permute-start.13 = (f32[96,2560]{1,0:T(8,128)}, f32[96,2560]{1,0:T(8,128)S(1)}, u32[]{:S(2)}, u32[]{:S(2)}) collective-permute-start(f32[96,2560]{1,0:T(8,128)} %get-tuple-element.101), channel_id=1, source_target_pairs={{0,16},{16,32},{32,48},{48,0},{1,17},{17,33},{33,49},{49,1},{2,18}... | collective-permute-start | bytes 2949128 | tf_op jit(solution)/shard_map/ppermute | solution.py:234
  97.9 33.7 %collective-permute-start.14 = (f32[96,2560]{1,0:T(8,128)}, f32[96,2560]{1,0:T(8,128)}, u32[]{:S(2)}, u32[]{:S(2)}) collective-permute-start(f32[96,2560]{1,0:T(8,128)} %get-tuple-element.102), channel_id=1, source_target_pairs={{0,48},{16,0},{32,16},{48,32},{1,49},{17,1},{33,17},{49,33},{2,50}... | collective-permute-start | bytes 2949128 | tf_op jit(solution)/shard_map/ppermute | solution.py:234
  105.5 32.1 %collective-permute-start.11 = (f32[8,8,2560]{2,1,0:T(8,128)S(1)}, f32[8,8,2560]{2,1,0:T(8,128)}, u32[]{:S(2)}, u32[]{:S(2)}) collective-permute-start(f32[8,8,2560]{2,1,0:T(8,128)S(1)} %slice.10), channel_id=1, source_target_pairs={{0,2},{2,4},{4,6},{6,0},{1,3},{3,5},{5,7},{7,1},{8,10},{10,12},{12... | collective-permute-start | bytes 1966088 | tf_op jit(solution)/shard_map/last_chunk/ppermute | solution.py:234
  105.8 31.8 %collective-permute-start.12 = (f32[8,8,2560]{2,1,0:T(8,128)S(1)}, f32[8,8,2560]{2,1,0:T(8,128)}, u32[]{:S(2)}, u32[]{:S(2)}) collective-permute-start(f32[8,8,2560]{2,1,0:T(8,128)S(1)} %slice.11), channel_id=1, source_target_pairs={{0,6},{2,0},{4,2},{6,4},{1,7},{3,1},{5,3},{7,5},{8,14},{10,8},{12,... | collective-permute-start | bytes 1966088 | tf_op jit(solution)/shard_map/last_chunk/ppermute | solution.py:234
  134.3 31.5 %collective-permute-start.17 = (f32[144,2560]{1,0:T(8,128)}, f32[144,2560]{1,0:T(8,128)}, u32[]{:S(2)}, u32[]{:S(2)}) collective-permute-start(f32[144,2560]{1,0:T(8,128)} %get-tuple-element.115), channel_id=1, source_target_pairs={{0,16},{16,32},{32,48},{48,0},{1,17},{17,33},{33,49},{49,1},{2,18}... | collective-permute-start | bytes 4423688 | tf_op jit(solution)/shard_map/ppermute | solution.py:234
  134.4 31.5 %collective-permute-start.18 = (f32[144,2560]{1,0:T(8,128)}, f32[144,2560]{1,0:T(8,128)}, u32[]{:S(2)}, u32[]{:S(2)}) collective-permute-start(f32[144,2560]{1,0:T(8,128)} %get-tuple-element.116), channel_id=1, source_target_pairs={{0,48},{16,0},{32,16},{48,32},{1,49},{17,1},{33,17},{49,33},{2,50}... | collective-permute-start | bytes 4423688 | tf_op jit(solution)/shard_map/ppermute | solution.py:234
  137.6 21.1 %all-to-all-start.1 = ((f32[8,16,2560]{2,1,0:T(8,128)}), f32[8,16,2560]{2,1,0:T(8,128)S(1)}, u32[]{:S(2)}, u32[]{:S(2)}) async-start(f32[8,16,2560]{2,1,0:T(8,128)} %get-tuple-element.120), calls=%async_computation.1 | async-start | bytes 2621440 | tf_op jit(solution)/shard_map/second_index/all_to_all | solution.py:296
  141.6 14.9 %collective-permute-start.19 = (f32[16,2560]{1,0:T(8,128)}, f32[16,2560]{1,0:T(8,128)}, u32[]{:S(2)}, u32[]{:S(2)}) collective-permute-start(f32[16,2560]{1,0:T(8,128)} %copy-done.29), channel_id=1, source_target_pairs={{0,64},{64,0},{1,65},{65,1},{2,66},{66,2},{3,67},{67,3},{4,68},{68... | collective-permute-start | bytes 491528 | tf_op jit(solution)/shard_map/ppermute | solution.py:234
  169.0 17.1 %collective-permute-start.22 = (f32[48,2560]{1,0:T(8,128)S(1)}, f32[48,2560]{1,0:T(8,128)S(1)}, u32[]{:S(2)}, u32[]{:S(2)}) collective-permute-start(f32[48,2560]{1,0:T(8,128)S(1)} %get-tuple-element.127), channel_id=1, source_target_pairs={{0,16},{16,32},{32,48},{48,0},{1,17},{17,33},{33,49},{49,1},{2,18}... | collective-permute-start | bytes 1474568 | tf_op jit(solution)/shard_map/ppermute | solution.py:234
  169.0 17.0 %collective-permute-start.23 = (f32[48,2560]{1,0:T(8,128)S(1)}, f32[48,2560]{1,0:T(8,128)S(1)}, u32[]{:S(2)}, u32[]{:S(2)}) collective-permute-start(f32[48,2560]{1,0:T(8,128)S(1)} %get-tuple-element.128), channel_id=1, source_target_pairs={{0,48},{16,0},{32,16},{48,32},{1,49},{17,1},{33,17},{49,33},{2,50}... | collective-permute-start | bytes 1474568 | tf_op jit(solution)/shard_map/ppermute | solution.py:234
  172.3 12.9 %collective-permute-start.15 = (f32[32,2560]{1,0:T(8,128)S(1)}, f32[32,2560]{1,0:T(8,128)S(1)}, u32[]{:S(2)}, u32[]{:S(2)}) collective-permute-start(f32[32,2560]{1,0:T(8,128)S(1)} %copy-done.35), channel_id=1, source_target_pairs={{0,16},{16,32},{32,48},{48,0},{1,17},{17,33},{33,49},{49,1},{2,18}... | collective-permute-start | bytes 983048 | tf_op jit(solution)/shard_map/ppermute | solution.py:234
  172.3 12.9 %collective-permute-start.16 = (f32[32,2560]{1,0:T(8,128)S(1)}, f32[32,2560]{1,0:T(8,128)S(1)}, u32[]{:S(2)}, u32[]{:S(2)}) collective-permute-start(f32[32,2560]{1,0:T(8,128)S(1)} %copy-done.34), channel_id=1, source_target_pairs={{0,48},{16,0},{32,16},{48,32},{1,49},{17,1},{33,17},{49,33},{2,50}... | collective-permute-start | bytes 983048 | tf_op jit(solution)/shard_map/ppermute | solution.py:234
  178.0 22.5 %collective-permute-start.26 = (f32[48,2560]{1,0:T(8,128)}, f32[48,2560]{1,0:T(8,128)}, u32[]{:S(2)}, u32[]{:S(2)}) collective-permute-start(f32[48,2560]{1,0:T(8,128)} %get-tuple-element.136), channel_id=1, source_target_pairs={{0,64},{64,0},{1,65},{65,1},{2,66},{66,2},{3,67},{67,3},{4,68},{68... | collective-permute-start | bytes 1474568 | tf_op jit(solution)/shard_map/ppermute | solution.py:234
  189.2 14.5 %collective-permute-start.25 = (f32[48,2560]{1,0:T(8,128)}, f32[48,2560]{1,0:T(8,128)}, u32[]{:S(2)}, u32[]{:S(2)}) collective-permute-start(f32[48,2560]{1,0:T(8,128)} %get-tuple-element.134), channel_id=1, source_target_pairs={{0,64},{64,0},{1,65},{65,1},{2,66},{66,2},{3,67},{67,3},{4,68},{68... | collective-permute-start | bytes 1474568 | tf_op jit(solution)/shard_map/ppermute | solution.py:234
  190.7 6.7 %collective-permute-start.20 = (f32[16,2560]{1,0:T(8,128)}, f32[16,2560]{1,0:T(8,128)S(1)}, u32[]{:S(2)}, u32[]{:S(2)}) collective-permute-start(f32[16,2560]{1,0:T(8,128)} %get-tuple-element.125), channel_id=1, source_target_pairs={{0,16},{16,32},{32,48},{48,0},{1,17},{17,33},{33,49},{49,1},{2,18}... | collective-permute-start | bytes 491528 | tf_op jit(solution)/shard_map/ppermute | solution.py:234
  191.5 6.0 %collective-permute-start.21 = (f32[16,2560]{1,0:T(8,128)}, f32[16,2560]{1,0:T(8,128)S(1)}, u32[]{:S(2)}, u32[]{:S(2)}) collective-permute-start(f32[16,2560]{1,0:T(8,128)} %get-tuple-element.126), channel_id=1, source_target_pairs={{0,48},{16,0},{32,16},{48,32},{1,49},{17,1},{33,17},{49,33},{2,50}... | collective-permute-start | bytes 491528 | tf_op jit(solution)/shard_map/ppermute | solution.py:234
  199.8 7.2 %collective-permute-start.24 = (f32[16,2560]{1,0:T(8,128)}, f32[16,2560]{1,0:T(8,128)S(1)}, u32[]{:S(2)}, u32[]{:S(2)}) collective-permute-start(f32[16,2560]{1,0:T(8,128)} %get-tuple-element.132), channel_id=1, source_target_pairs={{0,64},{64,0},{1,65},{65,1},{2,66},{66,2},{3,67},{67,3},{4,68},{68... | collective-permute-start | bytes 491528 | tf_op jit(solution)/shard_map/ppermute | solution.py:234
  208.0 5.1 %collective-permute-start.27 = (f32[2,64]{1,0:T(2,128)S(1)}, f32[2,64]{1,0:T(2,128)S(1)}, u32[]{:S(2)}, u32[]{:S(2)}) collective-permute-start(f32[2,64]{1,0:T(2,128)S(1)} %reshape.27), channel_id=1, source_target_pairs={{0,1},{1,0},{2,3},{3,2},{4,5},{5,4},{6,7},{7,6},{8,9},{9,8},{10,11... | collective-permute-start | bytes 1544 | tf_op jit(solution)/shard_map/bands/ppermute | solution.py:234
  213.1 3.6 %collective-permute-start.28 = (f32[2,64]{1,0:T(2,128)S(1)}, f32[2,64]{1,0:T(2,128)S(1)}, u32[]{:S(2)}, u32[]{:S(2)}) collective-permute-start(f32[2,64]{1,0:T(2,128)S(1)} %add.190), channel_id=1, source_target_pairs={{0,2},{2,0},{4,6},{6,4},{1,3},{3,1},{5,7},{7,5},{8,10},{10,8},{12,... | collective-permute-start | bytes 1544 | tf_op jit(solution)/shard_map/bands/ppermute | solution.py:320
  216.6 5.1 %collective-permute-start.29 = (f32[2,64]{1,0:T(2,128)S(1)}, f32[2,64]{1,0:T(2,128)S(1)}, u32[]{:S(2)}, u32[]{:S(2)}) collective-permute-start(f32[2,64]{1,0:T(2,128)S(1)} %add.191), channel_id=1, source_target_pairs={{0,4},{2,6},{4,0},{6,2},{1,5},{3,7},{5,1},{7,3},{8,12},{10,14},{12... | collective-permute-start | bytes 1544 | tf_op jit(solution)/shard_map/bands/ppermute | solution.py:320
  (37 other events, 182.5 us)

commit v2 on v1

v2 whole, which is shorter than its diff:
```python
import functools

import jax
import jax.numpy as jnp
from jax import lax
from jax.experimental import pallas as pl
from jax.experimental.pallas import tpu as pltpu
from jax.sharding import Mesh, PartitionSpec as P

NG = 20480
ROWS = 16
CHIP = 2560
HALF = 1280
TILE = 512
F32 = jnp.float32
BF16 = jnp.bfloat16
SIZES = {"xl": 2, "y": 4, "core": 2, "z": 4, "xh": 2}

OWNERS = ((0, 2), (1, 1), (1, 2), (0, 3), (0, 1), (1, 3), (0, 0), (1, 0))
WAVES = (((0, 0),), ((0, 1), (1, 0), (3, 0)), ((1, 1), (3, 1)), ((2, 0), (2, 1)))


def array(shape, dtype=F32):
    return jax.ShapeDtypeStruct(shape, dtype)


TOKEN = array((6656, CHIP))


def in_hbm(value):
    if isinstance(value, jax.ShapeDtypeStruct):
        return pltpu.HBM(value.shape, value.dtype)
    return pltpu.with_memory_space_constraint(value, pltpu.HBM)


KEPT = pl.BlockSpec(memory_space=pltpu.HBM)


def call(kernel, token, args, outs, in_specs, out_specs, grid, place=None, scratch=(), aliases=None, vmem=8):
    lead = 0 if place is None else 1
    n_in = lead + len(args)
    before = () if token is None else (token,)

    def body(*refs):
        rest = refs[n_in + len(before) :]
        kernel(*refs[:n_in], *rest[: len(outs)], *rest[len(outs) + 1 :])

    result = pl.pallas_call(
        body,
        grid_spec=pltpu.PrefetchScalarGridSpec(
            num_scalar_prefetch=lead,
            grid=grid,
            in_specs=[*in_specs, *(KEPT for _ in before)],
            out_specs=[*out_specs, KEPT],
            scratch_shapes=list(scratch),
        ),
        out_shape=[*outs, TOKEN],
        input_output_aliases=(aliases or {}) | ({n_in: len(outs)} if before else {}),
        compiler_params=pltpu.CompilerParams(vmem_limit_bytes=vmem << 20),
        cost_estimate=pl.CostEstimate(flops=1024, bytes_accessed=4096, transcendentals=0),
    )(*(() if place is None else (place,)), *args, *before)
    return result[:-1], result[-1]


def tie(values, token, space=pltpu.VMEM):
    n = len(values) + 1
    outs = [array(v.shape) for v in values]
    if space is pltpu.HBM:
        values, outs = [in_hbm(v) for v in values], [in_hbm(o) for o in outs]
    specs = [pl.BlockSpec(memory_space=space)] * len(values) + [KEPT]
    result = pl.pallas_call(
        lambda *refs: None,
        out_shape=[*outs, TOKEN],
        in_specs=specs,
        out_specs=specs,
        input_output_aliases={i: i for i in range(n)},
        compiler_params=pltpu.CompilerParams(vmem_limit_bytes=16 << 20),
        cost_estimate=pl.CostEstimate(flops=1024, bytes_accessed=4096, transcendentals=0),
    )(*values, token)
    return result[:-1], result[-1]


def cut_kernel(place_ref, x_ref, by_row_ref, by_col_ref):
    core = place_ref[0]
    for i in range(8):
        start = pl.multiple_of(i * CHIP + core * HALF, HALF)
        by_row_ref[i, :, :HALF] = x_ref[:, pl.ds(start, HALF)]
        start = pl.multiple_of(i * CHIP + (1 - core) * HALF, HALF)
        by_row_ref[i, :, HALF:] = x_ref[:, pl.ds(start, HALF)]
        by_col_ref[i] = x_ref[:, i * CHIP : (i + 1) * CHIP]


def split(value):
    high = value.astype(BF16)
    return high, (value - high.astype(F32)).astype(BF16)


def halve(w, token):
    def kernel(w_ref, halves_ref):
        halves_ref[0, 0], halves_ref[1, 0] = split(w_ref[...])

    return call(
        kernel,
        token,
        [w],
        [array((4, CHIP // TILE, HALF, TILE), BF16)],
        [pl.BlockSpec((HALF, TILE), lambda i, *_: (0, i))],
        [pl.BlockSpec((2, 1, HALF, TILE), lambda i, *_: (0, i, 0, 0))],
        (CHIP // TILE,),
        vmem=40,
    )


def screen_kernel(first, sizes, place_ref, *refs):
    n_x = sum(sizes)
    x_refs, halves_ref, rest = refs[:n_x], refs[n_x], refs[n_x + 1 :]
    up, down, left, *made, both_ref = rest[1:] if first else rest
    rows, n = 128 * len(sizes), ROWS * len(sizes)

    @pl.when(pl.program_id(0) == 0)
    def _():
        taken = 0
        for i, size in enumerate(sizes):
            for k in range(8):
                parts = [x_ref[place_ref[k]] for x_ref in x_refs[taken : taken + size]]
                high, low = split(parts[0] if size == 1 else jnp.concatenate(parts, axis=0))
                at = i * 128 + k * ROWS
                both_ref[at : at + ROWS, :] = high
                both_ref[rows + at : rows + at + ROWS, :] = low
            taken += size

    weights = [halves_ref[k, 0] for k in range(2 if first else 4)]
    if first:
        made[0][0, 0], made[0][1, 0] = split(rest[0][...])
        weights += [made[0][0, 0], made[0][1, 0]]
    total = None
    for part in range(2):
        high, low = weights[2 * part : 2 * part + 2]
        at = slice(part * HALF, (part + 1) * HALF)
        product = jnp.dot(both_ref[:, at], high, preferred_element_type=F32)
        product = product[:rows] + product[rows:]
        product += jnp.dot(both_ref[:rows, at], low, preferred_element_type=F32)
        total = product if total is None else total + product
    for i in range(len(sizes)):
        for k, (ref, group) in enumerate(
            ((up, 0), (up, 1), (down, 0), (down, 1), (left, 0), (left, 1), (left, 2), (left, 3))
        ):
            at = group * n + i * ROWS
            ref[at : at + ROWS, :] = total[i * 128 + k * ROWS : i * 128 + (k + 1) * ROWS]


def screen(owners, chunks, weights, token, spare=0):
    sizes = [len(c) for c in chunks]
    arrays = [a for c in chunks for a in c]
    n = ROWS * len(chunks)
    rows = (2 * n + spare, 2 * n + spare, 4 * n)
    first = len(weights) == 2
    halves = [pl.BlockSpec((k, 1, HALF, TILE), lambda i, *_, at=at: (at, i, 0, 0)) for k, at in ((4, 0), (2, 0), (2, 1))]
    return call(
        functools.partial(screen_kernel, first, sizes),
        token,
        [*arrays, *weights],
        [array((r, CHIP)) for r in rows[:2]] + [in_hbm(array((rows[2], CHIP)))] + [array(weights[0].shape, BF16)] * first,
        [pl.BlockSpec(a.shape, lambda i, *_: (0, 0, 0)) for a in arrays]
        + ([halves[1], pl.BlockSpec((HALF, TILE), lambda i, *_: (0, i))] if first else [halves[0]]),
        [pl.BlockSpec((r, TILE), lambda i, *_: (0, i)) for r in rows] + [halves[2]] * first,
        (CHIP // TILE,),
        place=owners,
        scratch=[pltpu.VMEM((16 * n, CHIP), BF16)],
        aliases={1 + len(arrays): 3} if first else {},
        vmem=40,
    )


def rows_from(*firsts):
    return [pl.BlockSpec((ROWS, CHIP), lambda i, *_, at=at // ROWS: (at + i, 0)) for at in firsts]


def pass_on(left, up, down, token, into=()):
    n = left.shape[0] // 4
    outs = [array(a.shape) for a in into] or [array((n, CHIP))] * 2

    def kernel(left_up, left_down, up, down, *rest):
        to_up, to_down = rest[-2:]
        to_up[...] = left_up[...] + up[...]
        to_down[...] = left_down[...] + down[...]

    return call(
        kernel,
        token,
        [in_hbm(left), in_hbm(left), up, down, *into],
        outs,
        rows_from(0, n, 0, 0) + [KEPT] * len(into),
        rows_from(outs[0].shape[0] - n, outs[0].shape[0] - n),
        (n // ROWS,),
        aliases={4: 0, 5: 1} if into else {},
    )


def turn(left, up, down, below, above, token, spare=0, into=()):
    n = left.shape[0] // 4
    passed = below.shape[0] - n
    outs = [array(a.shape) for a in into] or [array((n + spare, CHIP))] * 2
    at = outs[0].shape[0] - n if into else 0

    def kernel(stay, go, up, down, below, above, *rest):
        kept, out = rest[-2:]
        out[...] = go[...] + up[...] + above[...]
        kept[...] = stay[...] + down[...] + below[...]

    return call(
        kernel,
        token,
        [in_hbm(left), in_hbm(left), up, down, below, above, *into],
        [in_hbm(outs[0]), outs[1]],
        rows_from(2 * n, 3 * n, n, n, passed, passed) + [KEPT] * len(into),
        rows_from(at, at),
        (n // ROWS,),
        aliases={6: 0, 7: 1} if into else {},
    )


def finish(place, kept, across, block, held, token):
    def kernel(place_ref, kept, across, block, *rest):
        out, sums = rest[-2:]
        value = kept[...] + across[...]
        out[0] = value[:8]
        out[1] = value[8:]
        real, imag = block[0, :8, :], block[0, 8:, :]
        sums[0, :8, :] = jnp.sum(value[:8] * real + value[8:] * imag, axis=-1, keepdims=True)
        sums[0, 8:, :] = jnp.sum(value[:8] * imag - value[8:] * real, axis=-1, keepdims=True)

    return call(
        kernel,
        token,
        [in_hbm(kept), across, block, *held],
        [array((2, 64, CHIP)), array((8, ROWS, 1))],
        [pl.BlockSpec((ROWS, CHIP), lambda i, p, k=k: (k + i, 0)) for k in (0, 0)]
        + [pl.BlockSpec((1, ROWS, CHIP), lambda i, p: (p[i], 0, 0))]
        + [KEPT] * len(held),
        [
            pl.BlockSpec((2, 8, CHIP), lambda i, p: (0, p[i], 0)),
            pl.BlockSpec((1, ROWS, 1), lambda i, p: (p[i], 0, 0)),
        ],
        (kept.shape[0] // ROWS,),
        place=place,
        aliases={4: 0, 5: 1} if held else {},
    )


def move(value, axis, by):
    size = SIZES[axis]
    return lax.ppermute(value, axis, [(i, (i + by) % size) for i in range(size)])


def per_device(pair_elements, screened_w, occupied, freq_index):
    xl, y, core, z, xh = [lax.axis_index(a) for a in SIZES]
    other = move(screened_w, "core", 1)
    owners = jnp.stack([(xl + a) % 2 * 4 + (y + b) % 4 for a, b in OWNERS]).astype(jnp.int32)
    places = jnp.stack([(z + a) % 4 * 2 + (xh + b) % 2 for w in WAVES for a, b in w]).astype(jnp.int32)
    weight = 1.0 / (1.0 + 0.25 * freq_index[0].astype(F32))
    factor = weight * (0.5 - occupied.astype(F32)) * NG ** (-0.5)

    whole3 = pl.BlockSpec((8, ROWS, CHIP), lambda i, *_: (0, 0, 0))
    (by_row, by_col), token = call(
        cut_kernel,
        None,
        [in_hbm(pair_elements.reshape(ROWS, NG))],
        [in_hbm(array((8, ROWS, CHIP)))] * 2,
        [pl.BlockSpec((ROWS, NG), lambda i, *_: (0, 0))],
        [whole3] * 2,
        (1,),
        vmem=12,
        place=core.astype(jnp.int32).reshape(1),
    )
    with jax.named_scope("rows_to_their_plane_waves"):
        mine = lax.all_to_all(by_row, ("xl", "y"), 0, 0, tiled=True)
    halves, token = halve(screened_w, token)
    (mine,), token = tie([mine], token)
    chunk = {(0, 0): mine}
    with jax.named_scope("near_chunks"):
        chunk[3, 0] = move(mine, "z", 1)
        chunk[1, 0] = move(mine, "z", -1)
        chunk[0, 1] = move(mine, "xh", 1)

    (up0, down0, left0, *halves), token = screen(owners, [[mine]], [*halves, other], token)
    up0, down0 = move(up0, "y", 1), move(down0, "y", -1)

    with jax.named_scope("far_chunks"):
        (up0, down0), token = tie([up0, down0], token, pl.ANY)
        got, token = tie([chunk[c] for c in WAVES[1]], token, pl.ANY)
        chunk |= dict(zip(WAVES[1], got))
        chunk[3, 1] = move(chunk[0, 1], "z", 1)
        chunk[2, 0] = move(chunk[1, 0], "z", -1)
        chunk[1, 1] = move(chunk[1, 0], "xh", 1)

    (up1, down1, left1), token = screen(owners, [[in_hbm(chunk[c])] for c in WAVES[1]], halves, token, ROWS)
    (up1, down1), token = pass_on(left0, up0, down0, token, (up1, down1))
    up1, down1 = move(up1, "y", 1), move(down1, "y", -1)

    with jax.named_scope("last_chunk"):
        later = (*WAVES[2], (2, 0))
        got, token = tie([chunk[c] for c in later], token)
        chunk |= dict(zip(later, got))
        last = [move(chunk[3, 1][:, :8], "z", 1), move(chunk[1, 1][:, 8:], "z", -1)]

    (up2, down2, left2), token = screen(owners, [[chunk[c]] for c in WAVES[2]], halves, token, 3 * ROWS)
    last, token = tie(last, token)
    (by_col,), token = tie([by_col], token, pltpu.HBM)
    with jax.named_scope("second_index"):
        block = lax.all_to_all(by_col, ("z", "xh"), 0, 0, tiled=True)
    (up2, down2), token = pass_on(left1, up1, down1, token, (up2, down2))
    up2, down2 = move(up2, "y", 1), move(down2, "y", -1)
    begun, token = turn(left0, up0, down0, up1, down1, token, 3 * ROWS)

    (up3, down3, left3), token = screen(owners, [[chunk[2, 0]], last], halves, token)
    up3, down3 = move(up3, "y", 1), move(down3, "y", -1)
    (block,), token = tie([block], token, pltpu.HBM)
    (kept1, across1), token = turn(left1, up1, down1, up2, down2, token, 0, begun)
    across1 = move(across1, "xl", 1)
    (to_up, to_down), token = pass_on(left2, up2, down2, token)
    below2, above2 = move(to_up, "y", 1), move(to_down, "y", -1)
    (to_up, to_down), token = pass_on(left3, up3, down3, token)
    below3, above3 = move(to_up, "y", 1), move(to_down, "y", -1)
    (kept2, across2), token = turn(left2, up2, down2, below2, above2, token)
    across2 = move(across2, "xl", 1)
    (across1,), token = tie([across1], token)
    (kept3, across3), token = turn(left3, up3, down3, below3, above3, token)
    across3 = move(across3, "xl", 1)
    held, token = finish(places[:4], kept1, across1, block, (), token)
    held, token = finish(places[4:6], kept2, across2, block, held, token)
    (out, sums), token = finish(places[6:], kept3, across3, block, held, token)

    with jax.named_scope("bands"):
        sums = sums.reshape(8, 2, 8).transpose(1, 0, 2).reshape(2, 64)
        sums = sums + move(sums, "xh", 1)
        sums = (sums + move(sums, "z", 2)) + (move(sums, "z", 1) + move(sums, "z", -1))
    return out, sums * factor


def solution(mesh):
    fine = Mesh(mesh.devices.reshape(2, 4, 2, 4, 2), tuple(SIZES))
    row, col = ("xl", "y", "core"), ("z", "xh")
    return jax.shard_map(
        per_device,
        mesh=fine,
        in_specs=(P(None, row + col, None), P(row, col), P(row), P()),
        out_specs=(P(None, row, col), P(None, row)),
        check_vma=False,
    )
```

time: 223 us -> 209 us (0.937)
  waiting for transfers between devices: 40.9 us -> 29.1 us
  local copies, waits for them, and re-layouts: 18.1 us -> 8.27 us
  starting transfers between devices: 53.5 us -> 60.5 us
    unnamed x74 -> x22, local copies, waits for them, and re-layouts: 16.1 us -> 7.93 us
    ppermute x2 -> x0, waiting for transfers between devices: 7.71 us -> none  [per_device(): sums = sums + lax.ppermute(sums, 'z', list(enumerate(pairs)))]
    ppermute x28, starting transfers between devices: 43.8 us -> 48.3 us  [move(): lax.ppermute(value, axis, [(i, (i + by) % size) for i in range(size)])]
    all_to_all x1, starting transfers between devices: 4.01 us -> 6.66 us  [per_device(): block = lax.all_to_all(by_col, ('z', 'xh'), 0, 0, tiled=True)]
    pallas_call x18 -> x17, Pallas kernels: 107 us -> 108 us  [call(): pl.pallas_call(body, grid_spec=pltpu.PrefetchScalarGridSpec(num_scalar_pr...]
  transfers between devices with their start and end apart: 32 -> 30, of which waited for: 11 -> 12; matrix products, arithmetic and copies ran while one was open for 1% -> 0% of each run, Pallas kernels for 47% -> 51%
where the time goes in v2:
time: 209 us; the launch traced here: 208 us
  Pallas kernels  108 us (52%)
  starting transfers between devices  60.5 us (29%)
  waiting for transfers between devices  29.1 us (14%)
  local copies, waits for them, and re-layouts  8.27 us (4%)
    pallas_call x17, Pallas kernels, call(): pl.pallas_call(body, grid_spec=pltpu.PrefetchScalarGridSpec(num_scalar_pr...  108 us
    ppermute x28, starting transfers between devices, move(): lax.ppermute(value, axis, [(i, (i + by) % size) for i in range(size)])  48.3 us
    ppermute x28, waiting for transfers between devices, move(): lax.ppermute(value, axis, [(i, (i + by) % size) for i in range(size)])  21.9 us
    unnamed x22, local copies, waits for them, and re-layouts  7.93 us
    all_to_all x1, waiting for transfers between devices, per_device(): mine = lax.all_to_all(by_row, ('xl', 'y'), 0, 0, tiled=True)  7.28 us
    all_to_all x1, starting transfers between devices, per_device(): block = lax.all_to_all(by_col, ('z', 'xh'), 0, 0, tiled=True)  6.66 us
    all_to_all x1, starting transfers between devices, per_device(): mine = lax.all_to_all(by_row, ('xl', 'y'), 0, 0, tiled=True)  5.48 us
  transfers between devices with their start and end apart: 30, of which 12 were waited for; matrix products, arithmetic and copies ran while one was open for 0% of the time, Pallas kernels for 51%

profile of v2, /device:TPU:0, one launch (start us, length us, event | category | flops | bytes accessed | tf_op | source)
XLA Modules:
  0.0 208.4 jit_solution(9874170092833212007)
XLA Ops:
  0.7 3.0 %shard_map.59 = (f32[8,16,2560]{2,1,0:T(8,128)}, f32[8,16,2560]{2,1,0:T(8,128)}, f32[6656,2560]{1,0:T(8,128)}) custom-call(s32[1]{0:T(128)} %bitcast.10.refs_0_, f32[16,20480]{1,0:T(8,128)} %bitcast.20), custom_call_target="tpu_custom_call" | custom-call | flops 1024 | bytes 4096 | tf_op jit(solution)/shard_map/pallas_call | solution.py:48
  3.7 5.5 %all-to-all-start = ((f32[8,16,2560]{2,1,0:T(8,128)}), f32[8,16,2560]{2,1,0:T(8,128)S(1)}, u32[]{:S(2)}, u32[]{:S(2)}) async-start(f32[8,16,2560]{2,1,0:T(8,128)} %get-tuple-element.78), calls=%async_computation | async-start | bytes 2621440 | tf_op jit(solution)/shard_map/rows_to_their_plane_waves/all_to_all | solution.py:277
  9.2 4.7 %copy-done.2 = f32[1280,2560]{1,0:T(8,128)S(1)} copy-done((f32[1280,2560]{1,0:T(8,128)S(1)}, f32[1280,2560]{1,0:T(8,128)}, u32[]{:S(2)}) %copy-start.2) | copy-done | bytes 13107224
  13.9 6.3 %shard_map.60 = (bf16[4,5,1280,512]{3,2,1,0:T(8,128)(2,1)}, f32[6656,2560]{1,0:T(8,128)}) custom-call(f32[1280,2560]{1,0:T(8,128)S(1)} %copy-done.2, f32[6656,2560]{1,0:T(8,128)} %get-tuple-element.79.refs_1_), custom_call_target="tpu_custom_call", output_to_operand_aliasing={{1}: (1, {})} | custom-call | flops 1024 | bytes 4096 | tf_op jit(solution)/shard_map/pallas_call | solution.py:48
  20.2 7.3 %all-to-all-done.refs_0_ = f32[8,16,2560]{2,1,0:T(8,128)S(1)} async-done(((f32[8,16,2560]{2,1,0:T(8,128)}), f32[8,16,2560]{2,1,0:T(8,128)S(1)}, u32[]{:S(2)}, u32[]{:S(2)}) %all-to-all-start) | async-done | bytes 1310752 | tf_op jit(solution)/shard_map/rows_to_their_plane_waves/all_to_all | solution.py:277
  27.5 2.7 %collective-permute-start = (f32[8,16,2560]{2,1,0:T(8,128)S(1)}, f32[8,16,2560]{2,1,0:T(8,128)}, u32[]{:S(2)}, u32[]{:S(2)}) collective-permute-start(f32[8,16,2560]{2,1,0:T(8,128)S(1)} %get-tuple-element.81.refs_1_), channel_id=1, source_target_pairs={{0,1},{1,0},{2,3},{3,2},{4,5},{5,4},{6,7},{7,6},{8,9},{9,8},{10,11... | collective-permute-start | bytes 3932168 | tf_op jit(solution)/shard_map/near_chunks/ppermute | solution.py:253
  30.2 4.0 %collective-permute-start.1 = (f32[8,16,2560]{2,1,0:T(8,128)S(1)}, f32[8,16,2560]{2,1,0:T(8,128)}, u32[]{:S(2)}, u32[]{:S(2)}) collective-permute-start(f32[8,16,2560]{2,1,0:T(8,128)S(1)} %get-tuple-element.81.refs_1_), channel_id=1, source_target_pairs={{0,6},{2,0},{4,2},{6,4},{1,7},{3,1},{5,3},{7,5},{8,14},{10,8},{12,... | collective-permute-start | bytes 3932168 | tf_op jit(solution)/shard_map/near_chunks/ppermute | solution.py:253
  34.3 18.0 %shard_map.62 = (f32[32,2560]{1,0:T(8,128)S(1)}, f32[32,2560]{1,0:T(8,128)S(1)}, f32[64,2560]{1,0:T(8,128)}, bf16[4,5,1280,512]{3,2,1,0:T(8,128)(2,1)}, f32[6656,2560]{1,0:T(8,128)}) custom-call(s32[8]{0:T(128)S(1)} %stack.69.refs_0_, f32[8,16,2560]{2,1,0:T(8,128)S(1)} %get-tuple-element.81.refs_1_, ...), custom_call_target="tpu_custom_call", output_to_operand_aliasing={{3}: (2, {}), {4}: (4, {})} | custom-call | flops 1024 | bytes 4096 | tf_op jit(solution)/shard_map/pallas_call | solution.py:48
  53.2 2.4 %collective-permute-start.5 = (f32[32,2560]{1,0:T(8,128)S(1)}, f32[32,2560]{1,0:T(8,128)S(1)}, u32[]{:S(2)}, u32[]{:S(2)}) collective-permute-start(f32[32,2560]{1,0:T(8,128)S(1)} %get-tuple-element.85), channel_id=1, source_target_pairs={{0,48},{16,0},{32,16},{48,32},{1,49},{17,1},{33,17},{49,33},{2,50}... | collective-permute-start | bytes 983048 | tf_op jit(solution)/shard_map/ppermute | solution.py:253
  55.6 6.8 %collective-permute-done.4.refs_0_ = f32[32,2560]{1,0:T(8,128)S(1)} collective-permute-done((f32[32,2560]{1,0:T(8,128)S(1)}, f32[32,2560]{1,0:T(8,128)S(1)}, u32[]{:S(2)}, u32[]{:S(2)}) %collective-permute-start.4) | collective-permute-done | bytes 327712 | tf_op jit(solution)/shard_map/ppermute | solution.py:253
  62.4 2.9 %collective-permute-done.2.refs_2_ = f32[8,16,2560]{2,1,0:T(8,128)S(1)} collective-permute-done((f32[8,16,2560]{2,1,0:T(8,128)S(1)}, f32[8,16,2560]{2,1,0:T(8,128)S(1)}, u32[]{:S(2)}, u32[]{:S(2)}) %collective-permute-start.2) | collective-permute-done | bytes 1310752 | tf_op jit(solution)/shard_map/near_chunks/ppermute | solution.py:253
  67.2 3.2 %collective-permute-start.8 = (f32[8,16,2560]{2,1,0:T(8,128)}, f32[8,16,2560]{2,1,0:T(8,128)S(1)}, u32[]{:S(2)}, u32[]{:S(2)}) collective-permute-start(f32[8,16,2560]{2,1,0:T(8,128)} %get-tuple-element.88.refs_2_), channel_id=1, source_target_pairs={{0,6},{2,0},{4,2},{6,4},{1,7},{3,1},{5,3},{7,5},{8,14},{10,8},{12,... | collective-permute-start | bytes 3932168 | tf_op jit(solution)/shard_map/far_chunks/ppermute | solution.py:253
  70.4 21.7 %shard_map.63 = (f32[112,2560]{1,0:T(8,128)}, f32[112,2560]{1,0:T(8,128)}, f32[192,2560]{1,0:T(8,128)}, f32[6656,2560]{1,0:T(8,128)}) custom-call(s32[8]{0:T(128)S(1)} %stack.69.refs_0_, f32[8,16,2560]{2,1,0:T(8,128)} %get-tuple-element.89.refs_1_, f32[8,16,2560]{2,1,0:T(8,128)} %get-tuple-element.88.refs_2_, ...), custom_call_target="tpu_custom_call", output_to_operand_aliasing={{3}: (5, {})} | custom-call | flops 1024 | bytes 4096 | tf_op jit(solution)/shard_map/pallas_call | solution.py:48
  94.3 2.8 %collective-permute-start.12 = (f32[112,2560]{1,0:T(8,128)}, f32[112,2560]{1,0:T(8,128)}, u32[]{:S(2)}, u32[]{:S(2)}) collective-permute-start(f32[112,2560]{1,0:T(8,128)} %get-tuple-element.108), channel_id=1, source_target_pairs={{0,48},{16,0},{32,16},{48,32},{1,49},{17,1},{33,17},{49,33},{2,50}... | collective-permute-start | bytes 3440648 | tf_op jit(solution)/shard_map/ppermute | solution.py:253
  97.3 3.0 %collective-permute-start.10 = (f32[8,8,2560]{2,1,0:T(8,128)S(1)}, f32[8,8,2560]{2,1,0:T(8,128)S(1)}, u32[]{:S(2)}, u32[]{:S(2)}) collective-permute-start(f32[8,8,2560]{2,1,0:T(8,128)S(1)} %slice.13), channel_id=1, source_target_pairs={{0,6},{2,0},{4,2},{6,4},{1,7},{3,1},{5,3},{7,5},{8,14},{10,8},{12,... | collective-permute-start | bytes 1966088 | tf_op jit(solution)/shard_map/last_chunk/ppermute | solution.py:253
  100.5 16.4 %shard_map.65 = (f32[112,2560]{1,0:T(8,128)}, f32[112,2560]{1,0:T(8,128)}, f32[128,2560]{1,0:T(8,128)}, f32[6656,2560]{1,0:T(8,128)}) custom-call(s32[8]{0:T(128)S(1)} %stack.69.refs_0_, f32[8,16,2560]{2,1,0:T(8,128)S(1)} %get-tuple-element.102.refs_1_, f32[8,16,2560]{2,1,0:T(8,128)S(1)} %get-tuple-element.101.refs_2_, ...), custom_call_target="tpu_custom_call", output_to_operand_aliasing={{3}: (4, {})} | custom-call | flops 1024 | bytes 4096 | tf_op jit(solution)/shard_map/pallas_call | solution.py:48
  118.0 6.7 %all-to-all-start.1 = ((f32[8,16,2560]{2,1,0:T(8,128)}), f32[8,16,2560]{2,1,0:T(8,128)S(1)}, u32[]{:S(2)}, u32[]{:S(2)}) async-start(f32[8,16,2560]{2,1,0:T(8,128)} %get-tuple-element.125), calls=%async_computation.1 | async-start | bytes 2621440 | tf_op jit(solution)/shard_map/second_index/all_to_all | solution.py:311
  124.6 3.2 %shard_map.68 = (f32[112,2560]{1,0:T(8,128)}, f32[112,2560]{1,0:T(8,128)}, f32[6656,2560]{1,0:T(8,128)}) custom-call(f32[192,2560]{1,0:T(8,128)} %get-tuple-element.109.refs_0_.refs_1_, f32[192,2560]{1,0:T(8,128)} %get-tuple-element.109.refs_0_.refs_1_, ...), custom_call_target="tpu_custom_call", output_to_operand_aliasing={{0}: (4, {}), {1}: (5, {}), {2}: (6, {})} | custom-call | flops 1024 | bytes 4096 | tf_op jit(solution)/shard_map/pallas_call | solution.py:48
  128.0 3.1 %collective-permute-start.16 = (f32[112,2560]{1,0:T(8,128)}, f32[112,2560]{1,0:T(8,128)}, u32[]{:S(2)}, u32[]{:S(2)}) collective-permute-start(f32[112,2560]{1,0:T(8,128)} %get-tuple-element.122), channel_id=1, source_target_pairs={{0,48},{16,0},{32,16},{48,32},{1,49},{17,1},{33,17},{49,33},{2,50}... | collective-permute-start | bytes 3440648 | tf_op jit(solution)/shard_map/ppermute | solution.py:253
  133.1 16.1 %shard_map.70 = (f32[64,2560]{1,0:T(8,128)}, f32[64,2560]{1,0:T(8,128)}, f32[128,2560]{1,0:T(8,128)}, f32[6656,2560]{1,0:T(8,128)}) custom-call(s32[8]{0:T(128)S(1)} %stack.69.refs_0_, f32[8,16,2560]{2,1,0:T(8,128)S(1)} %copy-done.5, f32[8,8,2560]{2,1,0:T(8,128)S(1)} %copy-done.9, f32[8,8,2560]{2,1,0:T(8,128)S(1)} %copy-done.7, ...), custom_call_target="tpu_custom_call", output_to_operand_aliasing={{3}: (5, {})} | custom-call | flops 1024 | bytes 4096 | tf_op jit(solution)/shard_map/pallas_call | solution.py:48
  149.2 3.2 %collective-permute-start.14 = (f32[64,2560]{1,0:T(8,128)}, f32[64,2560]{1,0:T(8,128)}, u32[]{:S(2)}, u32[]{:S(2)}) collective-permute-start(f32[64,2560]{1,0:T(8,128)} %get-tuple-element.119), channel_id=1, source_target_pairs={{0,48},{16,0},{32,16},{48,32},{1,49},{17,1},{33,17},{49,33},{2,50}... | collective-permute-start | bytes 1966088 | tf_op jit(solution)/shard_map/ppermute | solution.py:253
  153.6 2.7 %collective-permute-done.15.refs_4_.refs_2_ = f32[112,2560]{1,0:T(8,128)} collective-permute-done((f32[112,2560]{1,0:T(8,128)}, f32[112,2560]{1,0:T(8,128)}, u32[]{:S(2)}, u32[]{:S(2)}) %collective-permute-start.15) | collective-permute-done | bytes 1146912 | tf_op jit(solution)/shard_map/ppermute | solution.py:253
  156.2 3.5 %shard_map.72 = (f32[64,2560]{1,0:T(8,128)}, f32[64,2560]{1,0:T(8,128)}, f32[6656,2560]{1,0:T(8,128)}) custom-call(f32[192,2560]{1,0:T(8,128)} %get-tuple-element.109.refs_0_.refs_1_, f32[192,2560]{1,0:T(8,128)} %get-tuple-element.109.refs_0_.refs_1_, ...), custom_call_target="tpu_custom_call", output_to_operand_aliasing={{0}: (6, {}), {1}: (7, {}), {2}: (8, {})} | custom-call | flops 1024 | bytes 4096 | tf_op jit(solution)/shard_map/pallas_call | solution.py:48
  164.5 2.9 %collective-permute-start.21 = (f32[32,2560]{1,0:T(8,128)}, f32[32,2560]{1,0:T(8,128)S(1)}, u32[]{:S(2)}, u32[]{:S(2)}) collective-permute-start(f32[32,2560]{1,0:T(8,128)} %get-tuple-element.134), channel_id=1, source_target_pairs={{0,48},{16,0},{32,16},{48,32},{1,49},{17,1},{33,17},{49,33},{2,50}... | collective-permute-start | bytes 983048 | tf_op jit(solution)/shard_map/ppermute | solution.py:253
  167.4 2.7 %collective-permute-done.13.refs_2_ = f32[64,2560]{1,0:T(8,128)S(1)} collective-permute-done((f32[64,2560]{1,0:T(8,128)}, f32[64,2560]{1,0:T(8,128)S(1)}, u32[]{:S(2)}, u32[]{:S(2)}) %collective-permute-start.13) | collective-permute-done | bytes 655392 | tf_op jit(solution)/shard_map/ppermute | solution.py:253
  171.6 3.2 %collective-permute-start.18 = (f32[32,2560]{1,0:T(8,128)S(1)}, f32[32,2560]{1,0:T(8,128)S(1)}, u32[]{:S(2)}, u32[]{:S(2)}) collective-permute-start(f32[32,2560]{1,0:T(8,128)S(1)} %get-tuple-element.131), channel_id=1, source_target_pairs={{0,48},{16,0},{32,16},{48,32},{1,49},{17,1},{33,17},{49,33},{2,50}... | collective-permute-start | bytes 983048 | tf_op jit(solution)/shard_map/ppermute | solution.py:253
  184.6 3.8 %shard_map.78 = (f32[2,64,2560]{2,1,0:T(8,128)}, f32[8,16,1]{2,1,0:T(8,128)S(1)}, f32[6656,2560]{1,0:T(8,128)}) custom-call(s32[4]{0:T(128)S(1)} %pad_add_fusion.2.refs_0_, f32[64,2560]{1,0:T(8,128)} %get-tuple-element.143.refs_1_, f32[64,2560]{1,0:T(8,128)S(1)} %get-tuple-element.144.refs_2_, ...), custom_call_target="tpu_custom_call", output_to_operand_aliasing={{2}: (4, {})} | custom-call | flops 1024 | bytes 4096 | tf_op jit(solution)/shard_map/pallas_call | solution.py:48
  188.6 2.3 %shard_map.79 = (f32[2,64,2560]{2,1,0:T(8,128)}, f32[8,16,1]{2,1,0:T(8,128)S(1)}, f32[6656,2560]{1,0:T(8,128)}) custom-call(s32[2]{0:T(128)S(1)} %pad_add_fusion.1.refs_0_, f32[32,2560]{1,0:T(8,128)} %get-tuple-element.141.refs_1_, f32[32,2560]{1,0:T(8,128)S(1)} %collective-permute-done.23.refs_2_, ...), custom_call_target="tpu_custom_call", output_to_operand_aliasing={{0}: (4, {}), {1}: (5, {}), {2}: (6, {})} | custom-call | flops 1024 | bytes 4096 | tf_op jit(solution)/shard_map/pallas_call | solution.py:48
  192.1 2.3 %shard_map.80 = (f32[2,64,2560]{2,1,0:T(8,128)}, f32[8,16,1]{2,1,0:T(8,128)S(1)}, f32[6656,2560]{1,0:T(8,128)}) custom-call(s32[2]{0:T(128)S(1)} %pad_add_fusion.refs_0_, f32[32,2560]{1,0:T(8,128)} %get-tuple-element.138.refs_1_, f32[32,2560]{1,0:T(8,128)S(1)} %collective-permute-done.22.refs_2_, ...), custom_call_target="tpu_custom_call", output_to_operand_aliasing={{0}: (4, {}), {1}: (5, {}), {2}: (6, {})} | custom-call | flops 1024 | bytes 4096 | tf_op jit(solution)/shard_map/pallas_call | solution.py:48
  194.7 3.3 %collective-permute-start.24 = (f32[2,64]{1,0:T(2,128)S(1)}, f32[2,64]{1,0:T(2,128)S(1)}, u32[]{:S(2)}, u32[]{:S(2)}) collective-permute-start(f32[2,64]{1,0:T(2,128)S(1)} %reshape.27), channel_id=1, source_target_pairs={{0,1},{1,0},{2,3},{3,2},{4,5},{5,4},{6,7},{7,6},{8,9},{9,8},{10,11... | collective-permute-start | bytes 1544 | tf_op jit(solution)/shard_map/bands/ppermute | solution.py:253
  199.8 3.2 %collective-permute-start.25 = (f32[2,64]{1,0:T(2,128)S(1)}, f32[2,64]{1,0:T(2,128)S(1)}, u32[]{:S(2)}, u32[]{:S(2)}) collective-permute-start(f32[2,64]{1,0:T(2,128)S(1)} %add.193), channel_id=1, source_target_pairs={{0,4},{2,6},{4,0},{6,2},{1,5},{3,7},{5,1},{7,3},{8,12},{10,14},{12... | collective-permute-start | bytes 1544 | tf_op jit(solution)/shard_map/bands/ppermute | solution.py:253
  203.6 2.7 %collective-permute-start.27 = (f32[2,64]{1,0:T(2,128)S(1)}, f32[2,64]{1,0:T(2,128)S(1)}, u32[]{:S(2)}, u32[]{:S(2)}) collective-permute-start(f32[2,64]{1,0:T(2,128)S(1)} %add.193), channel_id=1, source_target_pairs={{0,6},{2,0},{4,2},{6,4},{1,7},{3,1},{5,3},{7,5},{8,14},{10,8},{12,... | collective-permute-start | bytes 1544 | tf_op jit(solution)/shard_map/bands/ppermute | solution.py:253
  (88 shorter events, 31.2 us)
Async XLA Ops:
  0.6 33.7 %collective-permute-start.3 = (f32[1280,2560]{1,0:T(8,128)}, f32[1280,2560]{1,0:T(8,128)}, u32[]{:S(2)}, u32[]{:S(2)}) collective-permute-start(f32[1280,2560]{1,0:T(8,128)} %refs_0_.1), channel_id=1, source_target_pairs={{0,8},{8,0},{1,9},{9,1},{2,10},{10,2},{3,11},{11,3},{4,12},{12,4},... | collective-permute-start | bytes 39321608 | tf_op jit(solution)/shard_map/ppermute | solution.py:253
  3.7 23.7 %all-to-all-start = ((f32[8,16,2560]{2,1,0:T(8,128)}), f32[8,16,2560]{2,1,0:T(8,128)S(1)}, u32[]{:S(2)}, u32[]{:S(2)}) async-start(f32[8,16,2560]{2,1,0:T(8,128)} %get-tuple-element.78), calls=%async_computation | async-start | bytes 2621440 | tf_op jit(solution)/shard_map/rows_to_their_plane_waves/all_to_all | solution.py:277
  9.2 4.7 %copy-start.2 = (f32[1280,2560]{1,0:T(8,128)S(1)}, f32[1280,2560]{1,0:T(8,128)}, u32[]{:S(2)}) copy-start(f32[1280,2560]{1,0:T(8,128)} %refs_0_.1) | copy-start | bytes 39321604
  27.5 34.9 %collective-permute-start = (f32[8,16,2560]{2,1,0:T(8,128)S(1)}, f32[8,16,2560]{2,1,0:T(8,128)}, u32[]{:S(2)}, u32[]{:S(2)}) collective-permute-start(f32[8,16,2560]{2,1,0:T(8,128)S(1)} %get-tuple-element.81.refs_1_), channel_id=1, source_target_pairs={{0,1},{1,0},{2,3},{3,2},{4,5},{5,4},{6,7},{7,6},{8,9},{9,8},{10,11... | collective-permute-start | bytes 3932168 | tf_op jit(solution)/shard_map/near_chunks/ppermute | solution.py:253
  30.2 32.2 %collective-permute-start.1 = (f32[8,16,2560]{2,1,0:T(8,128)S(1)}, f32[8,16,2560]{2,1,0:T(8,128)}, u32[]{:S(2)}, u32[]{:S(2)}) collective-permute-start(f32[8,16,2560]{2,1,0:T(8,128)S(1)} %get-tuple-element.81.refs_1_), channel_id=1, source_target_pairs={{0,6},{2,0},{4,2},{6,4},{1,7},{3,1},{5,3},{7,5},{8,14},{10,8},{12,... | collective-permute-start | bytes 3932168 | tf_op jit(solution)/shard_map/near_chunks/ppermute | solution.py:253
  34.2 31.1 %collective-permute-start.2 = (f32[8,16,2560]{2,1,0:T(8,128)S(1)}, f32[8,16,2560]{2,1,0:T(8,128)S(1)}, u32[]{:S(2)}, u32[]{:S(2)}) collective-permute-start(f32[8,16,2560]{2,1,0:T(8,128)S(1)} %get-tuple-element.81.refs_1_), channel_id=1, source_target_pairs={{0,2},{2,4},{4,6},{6,0},{1,3},{3,5},{5,7},{7,1},{8,10},{10,12},{12... | collective-permute-start | bytes 3932168 | tf_op jit(solution)/shard_map/near_chunks/ppermute | solution.py:253
  52.4 10.0 %collective-permute-start.4 = (f32[32,2560]{1,0:T(8,128)S(1)}, f32[32,2560]{1,0:T(8,128)S(1)}, u32[]{:S(2)}, u32[]{:S(2)}) collective-permute-start(f32[32,2560]{1,0:T(8,128)S(1)} %get-tuple-element.84), channel_id=1, source_target_pairs={{0,16},{16,32},{32,48},{48,0},{1,17},{17,33},{33,49},{49,1},{2,18}... | collective-permute-start | bytes 983048 | tf_op jit(solution)/shard_map/ppermute | solution.py:253
  53.2 9.2 %collective-permute-start.5 = (f32[32,2560]{1,0:T(8,128)S(1)}, f32[32,2560]{1,0:T(8,128)S(1)}, u32[]{:S(2)}, u32[]{:S(2)}) collective-permute-start(f32[32,2560]{1,0:T(8,128)S(1)} %get-tuple-element.85), channel_id=1, source_target_pairs={{0,48},{16,0},{32,16},{48,32},{1,49},{17,1},{33,17},{49,33},{2,50}... | collective-permute-start | bytes 983048 | tf_op jit(solution)/shard_map/ppermute | solution.py:253
  66.4 30.7 %collective-permute-start.6 = (f32[8,16,2560]{2,1,0:T(8,128)}, f32[8,16,2560]{2,1,0:T(8,128)S(1)}, u32[]{:S(2)}, u32[]{:S(2)}) collective-permute-start(f32[8,16,2560]{2,1,0:T(8,128)} %get-tuple-element.88.refs_2_), channel_id=1, source_target_pairs={{0,1},{1,0},{2,3},{3,2},{4,5},{5,4},{6,7},{7,6},{8,9},{9,8},{10,11... | collective-permute-start | bytes 3932168 | tf_op jit(solution)/shard_map/far_chunks/ppermute | solution.py:253
  67.2 30.1 %collective-permute-start.7 = (f32[8,16,2560]{2,1,0:T(8,128)}, f32[8,16,2560]{2,1,0:T(8,128)S(1)}, u32[]{:S(2)}, u32[]{:S(2)}) collective-permute-start(f32[8,16,2560]{2,1,0:T(8,128)} %get-tuple-element.89.refs_1_), channel_id=1, source_target_pairs={{0,2},{2,4},{4,6},{6,0},{1,3},{3,5},{5,7},{7,1},{8,10},{10,12},{12... | collective-permute-start | bytes 3932168 | tf_op jit(solution)/shard_map/far_chunks/ppermute | solution.py:253
  67.2 30.1 %collective-permute-start.8 = (f32[8,16,2560]{2,1,0:T(8,128)}, f32[8,16,2560]{2,1,0:T(8,128)S(1)}, u32[]{:S(2)}, u32[]{:S(2)}) collective-permute-start(f32[8,16,2560]{2,1,0:T(8,128)} %get-tuple-element.88.refs_2_), channel_id=1, source_target_pairs={{0,6},{2,0},{4,2},{6,4},{1,7},{3,1},{5,3},{7,5},{8,14},{10,8},{12,... | collective-permute-start | bytes 3932168 | tf_op jit(solution)/shard_map/far_chunks/ppermute | solution.py:253
  93.8 30.8 %collective-permute-start.11 = (f32[112,2560]{1,0:T(8,128)}, f32[112,2560]{1,0:T(8,128)S(1)}, u32[]{:S(2)}, u32[]{:S(2)}) collective-permute-start(f32[112,2560]{1,0:T(8,128)} %get-tuple-element.107), channel_id=1, source_target_pairs={{0,16},{16,32},{32,48},{48,0},{1,17},{17,33},{33,49},{49,1},{2,18}... | collective-permute-start | bytes 3440648 | tf_op jit(solution)/shard_map/ppermute | solution.py:253
  94.3 30.3 %collective-permute-start.12 = (f32[112,2560]{1,0:T(8,128)}, f32[112,2560]{1,0:T(8,128)}, u32[]{:S(2)}, u32[]{:S(2)}) collective-permute-start(f32[112,2560]{1,0:T(8,128)} %get-tuple-element.108), channel_id=1, source_target_pairs={{0,48},{16,0},{32,16},{48,32},{1,49},{17,1},{33,17},{49,33},{2,50}... | collective-permute-start | bytes 3440648 | tf_op jit(solution)/shard_map/ppermute | solution.py:253
  97.3 19.5 %collective-permute-start.10 = (f32[8,8,2560]{2,1,0:T(8,128)S(1)}, f32[8,8,2560]{2,1,0:T(8,128)S(1)}, u32[]{:S(2)}, u32[]{:S(2)}) collective-permute-start(f32[8,8,2560]{2,1,0:T(8,128)S(1)} %slice.13), channel_id=1, source_target_pairs={{0,6},{2,0},{4,2},{6,4},{1,7},{3,1},{5,3},{7,5},{8,14},{10,8},{12,... | collective-permute-start | bytes 1966088 | tf_op jit(solution)/shard_map/last_chunk/ppermute | solution.py:253
  100.4 16.5 %collective-permute-start.9 = (f32[8,8,2560]{2,1,0:T(8,128)S(1)}, f32[8,8,2560]{2,1,0:T(8,128)S(1)}, u32[]{:S(2)}, u32[]{:S(2)}) collective-permute-start(f32[8,8,2560]{2,1,0:T(8,128)S(1)} %slice.12), channel_id=1, source_target_pairs={{0,2},{2,4},{4,6},{6,0},{1,3},{3,5},{5,7},{7,1},{8,10},{10,12},{12... | collective-permute-start | bytes 1966088 | tf_op jit(solution)/shard_map/last_chunk/ppermute | solution.py:253
  118.0 34.5 %all-to-all-start.1 = ((f32[8,16,2560]{2,1,0:T(8,128)}), f32[8,16,2560]{2,1,0:T(8,128)S(1)}, u32[]{:S(2)}, u32[]{:S(2)}) async-start(f32[8,16,2560]{2,1,0:T(8,128)} %get-tuple-element.125), calls=%async_computation.1 | async-start | bytes 2621440 | tf_op jit(solution)/shard_map/second_index/all_to_all | solution.py:311
  127.9 28.4 %collective-permute-start.15 = (f32[112,2560]{1,0:T(8,128)}, f32[112,2560]{1,0:T(8,128)}, u32[]{:S(2)}, u32[]{:S(2)}) collective-permute-start(f32[112,2560]{1,0:T(8,128)} %get-tuple-element.121), channel_id=1, source_target_pairs={{0,16},{16,32},{32,48},{48,0},{1,17},{17,33},{33,49},{49,1},{2,18}... | collective-permute-start | bytes 3440648 | tf_op jit(solution)/shard_map/ppermute | solution.py:253
  128.0 28.3 %collective-permute-start.16 = (f32[112,2560]{1,0:T(8,128)}, f32[112,2560]{1,0:T(8,128)}, u32[]{:S(2)}, u32[]{:S(2)}) collective-permute-start(f32[112,2560]{1,0:T(8,128)} %get-tuple-element.122), channel_id=1, source_target_pairs={{0,48},{16,0},{32,16},{48,32},{1,49},{17,1},{33,17},{49,33},{2,50}... | collective-permute-start | bytes 3440648 | tf_op jit(solution)/shard_map/ppermute | solution.py:253
  149.2 20.9 %collective-permute-start.13 = (f32[64,2560]{1,0:T(8,128)}, f32[64,2560]{1,0:T(8,128)S(1)}, u32[]{:S(2)}, u32[]{:S(2)}) collective-permute-start(f32[64,2560]{1,0:T(8,128)} %get-tuple-element.118), channel_id=1, source_target_pairs={{0,16},{16,32},{32,48},{48,0},{1,17},{17,33},{33,49},{49,1},{2,18}... | collective-permute-start | bytes 1966088 | tf_op jit(solution)/shard_map/ppermute | solution.py:253
  149.2 20.9 %collective-permute-start.14 = (f32[64,2560]{1,0:T(8,128)}, f32[64,2560]{1,0:T(8,128)}, u32[]{:S(2)}, u32[]{:S(2)}) collective-permute-start(f32[64,2560]{1,0:T(8,128)} %get-tuple-element.119), channel_id=1, source_target_pairs={{0,48},{16,0},{32,16},{48,32},{1,49},{17,1},{33,17},{49,33},{2,50}... | collective-permute-start | bytes 1966088 | tf_op jit(solution)/shard_map/ppermute | solution.py:253
  159.8 20.5 %collective-permute-start.19 = (f32[64,2560]{1,0:T(8,128)}, f32[64,2560]{1,0:T(8,128)S(1)}, u32[]{:S(2)}, u32[]{:S(2)}) collective-permute-start(f32[64,2560]{1,0:T(8,128)} %get-tuple-element.132), channel_id=1, source_target_pairs={{0,64},{64,0},{1,65},{65,1},{2,66},{66,2},{3,67},{67,3},{4,68},{68... | collective-permute-start | bytes 1966088 | tf_op jit(solution)/shard_map/ppermute | solution.py:253
  164.2 12.8 %collective-permute-start.20 = (f32[32,2560]{1,0:T(8,128)}, f32[32,2560]{1,0:T(8,128)S(1)}, u32[]{:S(2)}, u32[]{:S(2)}) collective-permute-start(f32[32,2560]{1,0:T(8,128)} %get-tuple-element.133), channel_id=1, source_target_pairs={{0,16},{16,32},{32,48},{48,0},{1,17},{17,33},{33,49},{49,1},{2,18}... | collective-permute-start | bytes 983048 | tf_op jit(solution)/shard_map/ppermute | solution.py:253
  164.5 12.5 %collective-permute-start.21 = (f32[32,2560]{1,0:T(8,128)}, f32[32,2560]{1,0:T(8,128)S(1)}, u32[]{:S(2)}, u32[]{:S(2)}) collective-permute-start(f32[32,2560]{1,0:T(8,128)} %get-tuple-element.134), channel_id=1, source_target_pairs={{0,48},{16,0},{32,16},{48,32},{1,49},{17,1},{33,17},{49,33},{2,50}... | collective-permute-start | bytes 983048 | tf_op jit(solution)/shard_map/ppermute | solution.py:253
  171.5 9.0 %collective-permute-start.17 = (f32[32,2560]{1,0:T(8,128)S(1)}, f32[32,2560]{1,0:T(8,128)S(1)}, u32[]{:S(2)}, u32[]{:S(2)}) collective-permute-start(f32[32,2560]{1,0:T(8,128)S(1)} %get-tuple-element.130), channel_id=1, source_target_pairs={{0,16},{16,32},{32,48},{48,0},{1,17},{17,33},{33,49},{49,1},{2,18}... | collective-permute-start | bytes 983048 | tf_op jit(solution)/shard_map/ppermute | solution.py:253
  171.6 8.9 %collective-permute-start.18 = (f32[32,2560]{1,0:T(8,128)S(1)}, f32[32,2560]{1,0:T(8,128)S(1)}, u32[]{:S(2)}, u32[]{:S(2)}) collective-permute-start(f32[32,2560]{1,0:T(8,128)S(1)} %get-tuple-element.131), channel_id=1, source_target_pairs={{0,48},{16,0},{32,16},{48,32},{1,49},{17,1},{33,17},{49,33},{2,50}... | collective-permute-start | bytes 983048 | tf_op jit(solution)/shard_map/ppermute | solution.py:253
  179.1 9.5 %collective-permute-start.23 = (f32[32,2560]{1,0:T(8,128)S(1)}, f32[32,2560]{1,0:T(8,128)S(1)}, u32[]{:S(2)}, u32[]{:S(2)}) collective-permute-start(f32[32,2560]{1,0:T(8,128)S(1)} %get-tuple-element.142), channel_id=1, source_target_pairs={{0,64},{64,0},{1,65},{65,1},{2,66},{66,2},{3,67},{67,3},{4,68},{68... | collective-permute-start | bytes 983048 | tf_op jit(solution)/shard_map/ppermute | solution.py:253
  182.6 9.5 %collective-permute-start.22 = (f32[32,2560]{1,0:T(8,128)S(1)}, f32[32,2560]{1,0:T(8,128)S(1)}, u32[]{:S(2)}, u32[]{:S(2)}) collective-permute-start(f32[32,2560]{1,0:T(8,128)S(1)} %get-tuple-element.139), channel_id=1, source_target_pairs={{0,64},{64,0},{1,65},{65,1},{2,66},{66,2},{3,67},{67,3},{4,68},{68... | collective-permute-start | bytes 983048 | tf_op jit(solution)/shard_map/ppermute | solution.py:253
  192.1 14.1 %copy-start.10 = (s32[64]{0:T(128)S(1)}, s32[64]{0:T(128)}, u32[]{:S(2)}) copy-start(s32[64]{0:T(128)} %param.6) | copy-start | bytes 772
  194.7 5.1 %collective-permute-start.24 = (f32[2,64]{1,0:T(2,128)S(1)}, f32[2,64]{1,0:T(2,128)S(1)}, u32[]{:S(2)}, u32[]{:S(2)}) collective-permute-start(f32[2,64]{1,0:T(2,128)S(1)} %reshape.27), channel_id=1, source_target_pairs={{0,1},{1,0},{2,3},{3,2},{4,5},{5,4},{6,7},{7,6},{8,9},{9,8},{10,11... | collective-permute-start | bytes 1544 | tf_op jit(solution)/shard_map/bands/ppermute | solution.py:253
  199.8 6.5 %collective-permute-start.25 = (f32[2,64]{1,0:T(2,128)S(1)}, f32[2,64]{1,0:T(2,128)S(1)}, u32[]{:S(2)}, u32[]{:S(2)}) collective-permute-start(f32[2,64]{1,0:T(2,128)S(1)} %add.193), channel_id=1, source_target_pairs={{0,4},{2,6},{4,0},{6,2},{1,5},{3,7},{5,1},{7,3},{8,12},{10,14},{12... | collective-permute-start | bytes 1544 | tf_op jit(solution)/shard_map/bands/ppermute | solution.py:253
  203.0 4.8 %collective-permute-start.26 = (f32[2,64]{1,0:T(2,128)S(1)}, f32[2,64]{1,0:T(2,128)S(1)}, u32[]{:S(2)}, u32[]{:S(2)}) collective-permute-start(f32[2,64]{1,0:T(2,128)S(1)} %add.193), channel_id=1, source_target_pairs={{0,2},{2,4},{4,6},{6,0},{1,3},{3,5},{5,7},{7,1},{8,10},{10,12},{12... | collective-permute-start | bytes 1544 | tf_op jit(solution)/shard_map/bands/ppermute | solution.py:253
  203.6 4.2 %collective-permute-start.27 = (f32[2,64]{1,0:T(2,128)S(1)}, f32[2,64]{1,0:T(2,128)S(1)}, u32[]{:S(2)}, u32[]{:S(2)}) collective-permute-start(f32[2,64]{1,0:T(2,128)S(1)} %add.193), channel_id=1, source_target_pairs={{0,6},{2,0},{4,2},{6,4},{1,7},{3,1},{5,3},{7,5},{8,14},{10,8},{12,... | collective-permute-start | bytes 1544 | tf_op jit(solution)/shard_map/bands/ppermute | solution.py:253
  (9 other events, 17.3 us)

commit v3 on v2

--- a/solution.py
+++ b/solution.py
@@ -111,10 +111,11 @@
     )
 
 
-def screen_kernel(first, sizes, place_ref, *refs):
+def screen_kernel(first, sizes, beside, n_beside, place_ref, *refs):
     n_x = sum(sizes)
     x_refs, halves_ref, rest = refs[:n_x], refs[n_x], refs[n_x + 1 :]
-    up, down, left, *made, both_ref = rest[1:] if first else rest
+    *rest, both_ref = rest
+    beside_refs, (up, down, left, *made) = rest[first : first + n_beside], rest[first + n_beside :]
     rows, n = 128 * len(sizes), ROWS * len(sizes)
 
     @pl.when(pl.program_id(0) == 0)
@@ -141,6 +142,8 @@
         product = product[:rows] + product[rows:]
         product += jnp.dot(both_ref[:rows, at], low, preferred_element_type=F32)
         total = product if total is None else total + product
+    if beside is not None:
+        beside(beside_refs, up, down, made)
     for i in range(len(sizes)):
         for k, (ref, group) in enumerate(
             ((up, 0), (up, 1), (down, 0), (down, 1), (left, 0), (left, 1), (left, 2), (left, 3))
@@ -149,7 +152,7 @@
             ref[at : at + ROWS, :] = total[i * 128 + k * ROWS : i * 128 + (k + 1) * ROWS]
 
 
-def screen(owners, chunks, weights, token, spare=0):
+def screen(owners, chunks, weights, token, spare=0, beside=None, beside_args=(), beside_specs=(), more=()):
     sizes = [len(c) for c in chunks]
     arrays = [a for c in chunks for a in c]
     n = ROWS * len(chunks)
@@ -157,19 +160,42 @@
     first = len(weights) == 2
     halves = [pl.BlockSpec((k, 1, HALF, TILE), lambda i, *_, at=at: (at, i, 0, 0)) for k, at in ((4, 0), (2, 0), (2, 1))]
     return call(
-        functools.partial(screen_kernel, first, sizes),
-        token,
-        [*arrays, *weights],
-        [array((r, CHIP)) for r in rows[:2]] + [in_hbm(array((rows[2], CHIP)))] + [array(weights[0].shape, BF16)] * first,
+        functools.partial(screen_kernel, first, sizes, beside, len(beside_args)),
+        token,
+        [*arrays, *weights, *beside_args],
+        [array((r, CHIP)) for r in rows[:2]]
+        + [in_hbm(array((rows[2], CHIP)))]
+        + [array(weights[0].shape, BF16)] * first
+        + [*more],
         [pl.BlockSpec(a.shape, lambda i, *_: (0, 0, 0)) for a in arrays]
-        + ([halves[1], pl.BlockSpec((HALF, TILE), lambda i, *_: (0, i))] if first else [halves[0]]),
-        [pl.BlockSpec((r, TILE), lambda i, *_: (0, i)) for r in rows] + [halves[2]] * first,
+        + ([halves[1], pl.BlockSpec((HALF, TILE), lambda i, *_: (0, i))] if first else [halves[0]])
+        + [*beside_specs],
+        [pl.BlockSpec((r, TILE), lambda i, *_: (0, i)) for r in rows]
+        + [halves[2]] * first
+        + [pl.BlockSpec((m.shape[0], TILE), lambda i, *_: (0, i)) for m in more],
         (CHIP // TILE,),
         place=owners,
         scratch=[pltpu.VMEM((16 * n, CHIP), BF16)],
         aliases={1 + len(arrays): 3} if first else {},
         vmem=40,
     )
+
+
+def tiles_from(*firsts):
+    return [pl.BlockSpec((ROWS, TILE), lambda i, *_, at=at // ROWS: (at, i)) for at in firsts]
+
+
+def pass_beside(refs, up, down, made):
+    left_up, left_down, from_up, from_down = refs
+    up[-ROWS:, :] = left_up[...] + from_up[...]
+    down[-ROWS:, :] = left_down[...] + from_down[...]
+
+
+def turn_beside(refs, up, down, made):
+    stay, go, from_up, from_down, below, above = refs
+    kept, out = made
+    kept[:ROWS, :] = stay[...] + from_down[...] + below[...]
+    out[:ROWS, :] = go[...] + from_up[...] + above[...]
 
 
 def rows_from(*firsts):
@@ -197,7 +223,7 @@
     )
 
 
-def turn(left, up, down, below, above, token, spare=0, into=()):
+def turn(left, up, down, below, above, token, spare=0, into=(), keep=in_hbm):
     n = left.shape[0] // 4
     passed = below.shape[0] - n
     outs = [array(a.shape) for a in into] or [array((n + spare, CHIP))] * 2
@@ -212,7 +238,7 @@
         kernel,
         token,
         [in_hbm(left), in_hbm(left), up, down, below, above, *into],
-        [in_hbm(outs[0]), outs[1]],
+        [keep(outs[0]), outs[1]],
         rows_from(2 * n, 3 * n, n, n, passed, passed) + [KEPT] * len(into),
         rows_from(at, at),
         (n // ROWS,),
@@ -220,7 +246,7 @@
     )
 
 
-def finish(place, kept, across, block, held, token):
+def finish(place, kept, across, block, held, token, keep=in_hbm):
     def kernel(place_ref, kept, across, block, *rest):
         out, sums = rest[-2:]
         value = kept[...] + across[...]
@@ -233,7 +259,7 @@
     return call(
         kernel,
         token,
-        [in_hbm(kept), across, block, *held],
+        [keep(kept), across, block, *held],
         [array((2, 64, CHIP)), array((8, ROWS, 1))],
         [pl.BlockSpec((ROWS, CHIP), lambda i, p, k=k: (k + i, 0)) for k in (0, 0)]
         + [pl.BlockSpec((1, ROWS, CHIP), lambda i, p: (p[i], 0, 0))]
@@ -294,8 +320,16 @@
         chunk[2, 0] = move(chunk[1, 0], "z", -1)
         chunk[1, 1] = move(chunk[1, 0], "xh", 1)
 
-    (up1, down1, left1), token = screen(owners, [[in_hbm(chunk[c])] for c in WAVES[1]], halves, token, ROWS)
-    (up1, down1), token = pass_on(left0, up0, down0, token, (up1, down1))
+    (up1, down1, left1), token = screen(
+        owners,
+        [[in_hbm(chunk[0, 1])], [in_hbm(chunk[1, 0])], [chunk[3, 0]]],
+        halves,
+        token,
+        ROWS,
+        pass_beside,
+        [in_hbm(left0), in_hbm(left0), up0, down0],
+        tiles_from(0, ROWS, 0, 0),
+    )
     up1, down1 = move(up1, "y", 1), move(down1, "y", -1)
 
     with jax.named_scope("last_chunk"):
@@ -306,30 +340,39 @@
 
     (up2, down2, left2), token = screen(owners, [[chunk[c]] for c in WAVES[2]], halves, token, 3 * ROWS)
     last, token = tie(last, token)
+    (up2, down2), token = pass_on(left1, up1, down1, token, (up2, down2))
+    up2, down2 = move(up2, "y", 1), move(down2, "y", -1)
+
     (by_col,), token = tie([by_col], token, pltpu.HBM)
     with jax.named_scope("second_index"):
         block = lax.all_to_all(by_col, ("z", "xh"), 0, 0, tiled=True)
-    (up2, down2), token = pass_on(left1, up1, down1, token, (up2, down2))
-    up2, down2 = move(up2, "y", 1), move(down2, "y", -1)
-    begun, token = turn(left0, up0, down0, up1, down1, token, 3 * ROWS)
-
-    (up3, down3, left3), token = screen(owners, [[chunk[2, 0]], last], halves, token)
+    (up3, down3, left3, *begun), token = screen(
+        owners,
+        [[in_hbm(chunk[2, 0])], [in_hbm(a) for a in last]],
+        halves,
+        token,
+        0,
+        turn_beside,
+        [in_hbm(left0), in_hbm(left0), up0, down0, up1, down1],
+        tiles_from(2 * ROWS, 3 * ROWS, ROWS, ROWS, 6 * ROWS, 6 * ROWS),
+        [in_hbm(array((4 * ROWS, CHIP))), array((4 * ROWS, CHIP))],
+    )
     up3, down3 = move(up3, "y", 1), move(down3, "y", -1)
+    (kept1, across1), token = turn(left1, up1, down1, up2, down2, token, 0, begun)
     (block,), token = tie([block], token, pltpu.HBM)
-    (kept1, across1), token = turn(left1, up1, down1, up2, down2, token, 0, begun)
     across1 = move(across1, "xl", 1)
     (to_up, to_down), token = pass_on(left2, up2, down2, token)
     below2, above2 = move(to_up, "y", 1), move(to_down, "y", -1)
     (to_up, to_down), token = pass_on(left3, up3, down3, token)
     below3, above3 = move(to_up, "y", 1), move(to_down, "y", -1)
-    (kept2, across2), token = turn(left2, up2, down2, below2, above2, token)
+    (kept2, across2), token = turn(left2, up2, down2, below2, above2, token, keep=lambda a: a)
     across2 = move(across2, "xl", 1)
     (across1,), token = tie([across1], token)
-    (kept3, across3), token = turn(left3, up3, down3, below3, above3, token)
+    (kept3, across3), token = turn(left3, up3, down3, below3, above3, token, keep=lambda a: a)
     across3 = move(across3, "xl", 1)
     held, token = finish(places[:4], kept1, across1, block, (), token)
-    held, token = finish(places[4:6], kept2, across2, block, held, token)
-    (out, sums), token = finish(places[6:], kept3, across3, block, held, token)
+    held, token = finish(places[4:6], kept2, across2, block, held, token, lambda a: a)
+    (out, sums), token = finish(places[6:], kept3, across3, block, held, token, lambda a: a)
 
     with jax.named_scope("bands"):
         sums = sums.reshape(8, 2, 8).transpose(1, 0, 2).reshape(2, 64)

time: 209 us -> 202 us (0.967)
  Pallas kernels: 108 us -> 102 us
  starting transfers between devices: 60.5 us -> 57.4 us
  waiting for transfers between devices: 29.1 us -> 31.3 us
    pallas_call x17 -> x15, Pallas kernels: 108 us -> 102 us  [call(): pl.pallas_call(body, grid_spec=pltpu.PrefetchScalarGridSpec(num_scalar_pr...]
    ppermute x28, starting transfers between devices: 48.3 us -> 46.1 us  [move(): lax.ppermute(value, axis, [(i, (i + by) % size) for i in range(size)])]
    ppermute x28, waiting for transfers between devices: 21.9 us -> 24 us  [move(): lax.ppermute(value, axis, [(i, (i + by) % size) for i in range(size)])]
    unnamed x22 -> x18, local copies, waits for them, and re-layouts: 7.93 us -> 7.06 us
  transfers between devices with their start and end apart: 30 -> 30, of which waited for: 12 -> 13; matrix products, arithmetic and copies ran while one was open for 0% -> 0% of each run, Pallas kernels for 51% -> 49%
where the time goes in v3:
time: 202 us; the launch traced here: 201 us
  Pallas kernels  102 us (50%)
  starting transfers between devices  57.4 us (28%)
  waiting for transfers between devices  31.3 us (15%)
  local copies, waits for them, and re-layouts  7.39 us (4%)
    pallas_call x15, Pallas kernels, call(): pl.pallas_call(body, grid_spec=pltpu.PrefetchScalarGridSpec(num_scalar_pr...  102 us
    ppermute x28, starting transfers between devices, move(): lax.ppermute(value, axis, [(i, (i + by) % size) for i in range(size)])  46.1 us
    ppermute x28, waiting for transfers between devices, move(): lax.ppermute(value, axis, [(i, (i + by) % size) for i in range(size)])  24 us
    all_to_all x1, waiting for transfers between devices, per_device(): mine = lax.all_to_all(by_row, ('xl', 'y'), 0, 0, tiled=True)  7.29 us
    unnamed x18, local copies, waits for them, and re-layouts  7.06 us
    all_to_all x1, starting transfers between devices, per_device(): block = lax.all_to_all(by_col, ('z', 'xh'), 0, 0, tiled=True)  5.86 us
    all_to_all x1, starting transfers between devices, per_device(): mine = lax.all_to_all(by_row, ('xl', 'y'), 0, 0, tiled=True)  5.48 us
  transfers between devices with their start and end apart: 30, of which 13 were waited for; matrix products, arithmetic and copies ran while one was open for 0% of the time, Pallas kernels for 49%

profile of v3, /device:TPU:0, one launch (start us, length us, event | category | flops | bytes accessed | tf_op | source)
XLA Modules:
  0.0 201.0 jit_solution(2166869456289371809)
XLA Ops:
  0.7 3.0 %shard_map.59 = (f32[8,16,2560]{2,1,0:T(8,128)}, f32[8,16,2560]{2,1,0:T(8,128)}, f32[6656,2560]{1,0:T(8,128)}) custom-call(s32[1]{0:T(128)} %bitcast.10.refs_0_, f32[16,20480]{1,0:T(8,128)} %bitcast.20), custom_call_target="tpu_custom_call" | custom-call | flops 1024 | bytes 4096 | tf_op jit(solution)/shard_map/pallas_call | solution.py:48
  3.7 5.5 %all-to-all-start = ((f32[8,16,2560]{2,1,0:T(8,128)}), f32[8,16,2560]{2,1,0:T(8,128)S(1)}, u32[]{:S(2)}, u32[]{:S(2)}) async-start(f32[8,16,2560]{2,1,0:T(8,128)} %get-tuple-element.74), calls=%async_computation | async-start | bytes 2621440 | tf_op jit(solution)/shard_map/rows_to_their_plane_waves/all_to_all | solution.py:303
  9.2 4.7 %copy-done.2 = f32[1280,2560]{1,0:T(8,128)S(1)} copy-done((f32[1280,2560]{1,0:T(8,128)S(1)}, f32[1280,2560]{1,0:T(8,128)}, u32[]{:S(2)}) %copy-start.2) | copy-done | bytes 13107224
  13.9 6.2 %shard_map.60 = (bf16[4,5,1280,512]{3,2,1,0:T(8,128)(2,1)}, f32[6656,2560]{1,0:T(8,128)}) custom-call(f32[1280,2560]{1,0:T(8,128)S(1)} %copy-done.2, f32[6656,2560]{1,0:T(8,128)} %get-tuple-element.75.refs_1_), custom_call_target="tpu_custom_call", output_to_operand_aliasing={{1}: (1, {})} | custom-call | flops 1024 | bytes 4096 | tf_op jit(solution)/shard_map/pallas_call | solution.py:48
  20.2 7.3 %all-to-all-done.refs_0_ = f32[8,16,2560]{2,1,0:T(8,128)S(1)} async-done(((f32[8,16,2560]{2,1,0:T(8,128)}), f32[8,16,2560]{2,1,0:T(8,128)S(1)}, u32[]{:S(2)}, u32[]{:S(2)}) %all-to-all-start) | async-done | bytes 1310752 | tf_op jit(solution)/shard_map/rows_to_their_plane_waves/all_to_all | solution.py:303
  27.5 2.7 %collective-permute-start = (f32[8,16,2560]{2,1,0:T(8,128)S(1)}, f32[8,16,2560]{2,1,0:T(8,128)}, u32[]{:S(2)}, u32[]{:S(2)}) collective-permute-start(f32[8,16,2560]{2,1,0:T(8,128)S(1)} %get-tuple-element.77.refs_1_), channel_id=1, source_target_pairs={{0,1},{1,0},{2,3},{3,2},{4,5},{5,4},{6,7},{7,6},{8,9},{9,8},{10,11... | collective-permute-start | bytes 3932168 | tf_op jit(solution)/shard_map/near_chunks/ppermute | solution.py:279
  30.2 4.0 %collective-permute-start.1 = (f32[8,16,2560]{2,1,0:T(8,128)S(1)}, f32[8,16,2560]{2,1,0:T(8,128)}, u32[]{:S(2)}, u32[]{:S(2)}) collective-permute-start(f32[8,16,2560]{2,1,0:T(8,128)S(1)} %get-tuple-element.77.refs_1_), channel_id=1, source_target_pairs={{0,6},{2,0},{4,2},{6,4},{1,7},{3,1},{5,3},{7,5},{8,14},{10,8},{12,... | collective-permute-start | bytes 3932168 | tf_op jit(solution)/shard_map/near_chunks/ppermute | solution.py:279
  34.3 18.0 %shard_map.62 = (f32[32,2560]{1,0:T(8,128)S(1)}, f32[32,2560]{1,0:T(8,128)S(1)}, f32[64,2560]{1,0:T(8,128)}, bf16[4,5,1280,512]{3,2,1,0:T(8,128)(2,1)}, f32[6656,2560]{1,0:T(8,128)}) custom-call(s32[8]{0:T(128)S(1)} %stack.69.refs_0_, f32[8,16,2560]{2,1,0:T(8,128)S(1)} %get-tuple-element.77.refs_1_, ...), custom_call_target="tpu_custom_call", output_to_operand_aliasing={{3}: (2, {}), {4}: (4, {})} | custom-call | flops 1024 | bytes 4096 | tf_op jit(solution)/shard_map/pallas_call | solution.py:48
  53.2 2.4 %collective-permute-start.5 = (f32[32,2560]{1,0:T(8,128)S(1)}, f32[32,2560]{1,0:T(8,128)S(1)}, u32[]{:S(2)}, u32[]{:S(2)}) collective-permute-start(f32[32,2560]{1,0:T(8,128)S(1)} %get-tuple-element.81), channel_id=1, source_target_pairs={{0,48},{16,0},{32,16},{48,32},{1,49},{17,1},{33,17},{49,33},{2,50}... | collective-permute-start | bytes 983048 | tf_op jit(solution)/shard_map/ppermute | solution.py:279
  55.6 6.8 %collective-permute-done.4.refs_0_ = f32[32,2560]{1,0:T(8,128)S(1)} collective-permute-done((f32[32,2560]{1,0:T(8,128)S(1)}, f32[32,2560]{1,0:T(8,128)S(1)}, u32[]{:S(2)}, u32[]{:S(2)}) %collective-permute-start.4) | collective-permute-done | bytes 327712 | tf_op jit(solution)/shard_map/ppermute | solution.py:279
  62.4 2.9 %collective-permute-done.2.refs_2_ = f32[8,16,2560]{2,1,0:T(8,128)S(1)} collective-permute-done((f32[8,16,2560]{2,1,0:T(8,128)S(1)}, f32[8,16,2560]{2,1,0:T(8,128)S(1)}, u32[]{:S(2)}, u32[]{:S(2)}) %collective-permute-start.2) | collective-permute-done | bytes 1310752 | tf_op jit(solution)/shard_map/near_chunks/ppermute | solution.py:279
  66.1 3.2 %collective-permute-start.8 = (f32[8,16,2560]{2,1,0:T(8,128)}, f32[8,16,2560]{2,1,0:T(8,128)S(1)}, u32[]{:S(2)}, u32[]{:S(2)}) collective-permute-start(f32[8,16,2560]{2,1,0:T(8,128)} %get-tuple-element.84.refs_2_), channel_id=1, source_target_pairs={{0,6},{2,0},{4,2},{6,4},{1,7},{3,1},{5,3},{7,5},{8,14},{10,8},{12,... | collective-permute-start | bytes 3932168 | tf_op jit(solution)/shard_map/far_chunks/ppermute | solution.py:279
  69.4 21.4 %shard_map.63 = (f32[112,2560]{1,0:T(8,128)S(1)}, f32[112,2560]{1,0:T(8,128)S(1)}, f32[192,2560]{1,0:T(8,128)}, f32[6656,2560]{1,0:T(8,128)}) custom-call(s32[8]{0:T(128)S(1)} %stack.69.refs_0_, f32[8,16,2560]{2,1,0:T(8,128)} %get-tuple-element.85.refs_1_, f32[8,16,2560]{2,1,0:T(8,128)} %get-tuple-element.84.refs_2_, ...), custom_call_target="tpu_custom_call", output_to_operand_aliasing={{3}: (9, {})} | custom-call | flops 1024 | bytes 4096 | tf_op jit(solution)/shard_map/pallas_call | solution.py:48
  91.2 2.8 %collective-permute-start.12 = (f32[112,2560]{1,0:T(8,128)S(1)}, f32[112,2560]{1,0:T(8,128)S(1)}, u32[]{:S(2)}, u32[]{:S(2)}) collective-permute-start(f32[112,2560]{1,0:T(8,128)S(1)} %get-tuple-element.101), channel_id=1, source_target_pairs={{0,48},{16,0},{32,16},{48,32},{1,49},{17,1},{33,17},{49,33},{2,50}... | collective-permute-start | bytes 3440648 | tf_op jit(solution)/shard_map/ppermute | solution.py:279
  96.3 3.0 %collective-permute-start.10 = (f32[8,8,2560]{2,1,0:T(8,128)S(1)}, f32[8,8,2560]{2,1,0:T(8,128)S(1)}, u32[]{:S(2)}, u32[]{:S(2)}) collective-permute-start(f32[8,8,2560]{2,1,0:T(8,128)S(1)} %slice.13), channel_id=1, source_target_pairs={{0,6},{2,0},{4,2},{6,4},{1,7},{3,1},{5,3},{7,5},{8,14},{10,8},{12,... | collective-permute-start | bytes 1966088 | tf_op jit(solution)/shard_map/last_chunk/ppermute | solution.py:279
  99.4 16.4 %shard_map.64 = (f32[112,2560]{1,0:T(8,128)}, f32[112,2560]{1,0:T(8,128)}, f32[128,2560]{1,0:T(8,128)}, f32[6656,2560]{1,0:T(8,128)}) custom-call(s32[8]{0:T(128)S(1)} %stack.69.refs_0_, f32[8,16,2560]{2,1,0:T(8,128)S(1)} %get-tuple-element.95.refs_1_, f32[8,16,2560]{2,1,0:T(8,128)S(1)} %get-tuple-element.94.refs_2_, ...), custom_call_target="tpu_custom_call", output_to_operand_aliasing={{3}: (4, {})} | custom-call | flops 1024 | bytes 4096 | tf_op jit(solution)/shard_map/pallas_call | solution.py:48
  116.6 3.5 %shard_map.66 = (f32[112,2560]{1,0:T(8,128)}, f32[112,2560]{1,0:T(8,128)}, f32[6656,2560]{1,0:T(8,128)}) custom-call(f32[192,2560]{1,0:T(8,128)} %get-tuple-element.103.refs_0_.refs_1_, f32[192,2560]{1,0:T(8,128)} %get-tuple-element.103.refs_0_.refs_1_, ...), custom_call_target="tpu_custom_call", output_to_operand_aliasing={{0}: (4, {}), {1}: (5, {}), {2}: (6, {})} | custom-call | flops 1024 | bytes 4096 | tf_op jit(solution)/shard_map/pallas_call | solution.py:48
  120.1 3.2 %collective-permute-start.16 = (f32[112,2560]{1,0:T(8,128)}, f32[112,2560]{1,0:T(8,128)}, u32[]{:S(2)}, u32[]{:S(2)}) collective-permute-start(f32[112,2560]{1,0:T(8,128)} %get-tuple-element.114), channel_id=1, source_target_pairs={{0,48},{16,0},{32,16},{48,32},{1,49},{17,1},{33,17},{49,33},{2,50}... | collective-permute-start | bytes 3440648 | tf_op jit(solution)/shard_map/ppermute | solution.py:279
  123.4 5.9 %all-to-all-start.1 = ((f32[8,16,2560]{2,1,0:T(8,128)}), f32[8,16,2560]{2,1,0:T(8,128)S(1)}, u32[]{:S(2)}, u32[]{:S(2)}) async-start(f32[8,16,2560]{2,1,0:T(8,128)} %get-tuple-element.115), calls=%async_computation.1 | async-start | bytes 2621440 | tf_op jit(solution)/shard_map/second_index/all_to_all | solution.py:348
  130.5 16.9 %shard_map.68 = (f32[64,2560]{1,0:T(8,128)}, f32[64,2560]{1,0:T(8,128)}, f32[128,2560]{1,0:T(8,128)}, f32[64,2560]{1,0:T(8,128)}, f32[64,2560]{1,0:T(8,128)}, /*index=5*/f32[6656,2560]{1,0:T(8,128)}) custom-call(s32[8]{0:T(128)S(1)} %stack.69.refs_0_, f32[8,16,2560]{2,1,0:T(8,128)} %copy-done.5, ...), custom_call_target="tpu_custom_call", output_to_operand_aliasing={{5}: (11, {})} | custom-call | flops 1024 | bytes 4096 | tf_op jit(solution)/shard_map/pallas_call | solution.py:48
  147.4 3.2 %collective-permute-start.14 = (f32[64,2560]{1,0:T(8,128)}, f32[64,2560]{1,0:T(8,128)}, u32[]{:S(2)}, u32[]{:S(2)}) collective-permute-start(f32[64,2560]{1,0:T(8,128)} %get-tuple-element.111), channel_id=1, source_target_pairs={{0,48},{16,0},{32,16},{48,32},{1,49},{17,1},{33,17},{49,33},{2,50}... | collective-permute-start | bytes 1966088 | tf_op jit(solution)/shard_map/ppermute | solution.py:279
  150.7 3.4 %shard_map.69 = (f32[64,2560]{1,0:T(8,128)}, f32[64,2560]{1,0:T(8,128)}, f32[6656,2560]{1,0:T(8,128)}) custom-call(f32[192,2560]{1,0:T(8,128)} %get-tuple-element.103.refs_0_.refs_1_, f32[192,2560]{1,0:T(8,128)} %get-tuple-element.103.refs_0_.refs_1_, ...), custom_call_target="tpu_custom_call", output_to_operand_aliasing={{0}: (6, {}), {1}: (7, {}), {2}: (8, {})} | custom-call | flops 1024 | bytes 4096 | tf_op jit(solution)/shard_map/pallas_call | solution.py:48
  156.0 2.1 %shard_map.71 = (f32[32,2560]{1,0:T(8,128)}, f32[32,2560]{1,0:T(8,128)S(1)}, f32[6656,2560]{1,0:T(8,128)}) custom-call(f32[128,2560]{1,0:T(8,128)} %get-tuple-element.112.refs_0_.refs_1_, f32[128,2560]{1,0:T(8,128)} %get-tuple-element.112.refs_0_.refs_1_, f32[112,2560]{1,0:T(8,128)} %collective-permute-done.15.refs_4_.refs_2_, ...), custom_call_target="tpu_custom_call", output_to_operand_aliasing={{2}: (4, {})} | custom-call | flops 1024 | bytes 4096 | tf_op jit(solution)/shard_map/pallas_call | solution.py:48
  158.1 3.2 %collective-permute-start.21 = (f32[32,2560]{1,0:T(8,128)S(1)}, f32[32,2560]{1,0:T(8,128)S(1)}, u32[]{:S(2)}, u32[]{:S(2)}) collective-permute-start(f32[32,2560]{1,0:T(8,128)S(1)} %get-tuple-element.126), channel_id=1, source_target_pairs={{0,48},{16,0},{32,16},{48,32},{1,49},{17,1},{33,17},{49,33},{2,50}... | collective-permute-start | bytes 983048 | tf_op jit(solution)/shard_map/ppermute | solution.py:279
  161.3 3.8 %collective-permute-done.13.refs_2_ = f32[64,2560]{1,0:T(8,128)S(1)} collective-permute-done((f32[64,2560]{1,0:T(8,128)}, f32[64,2560]{1,0:T(8,128)S(1)}, u32[]{:S(2)}, u32[]{:S(2)}) %collective-permute-start.13) | collective-permute-done | bytes 655392 | tf_op jit(solution)/shard_map/ppermute | solution.py:279
  165.1 2.1 %shard_map.72 = (f32[32,2560]{1,0:T(8,128)}, f32[32,2560]{1,0:T(8,128)}, f32[6656,2560]{1,0:T(8,128)}) custom-call(f32[128,2560]{1,0:T(8,128)} %get-tuple-element.109.refs_0_.refs_1_, f32[128,2560]{1,0:T(8,128)} %get-tuple-element.109.refs_0_.refs_1_, f32[64,2560]{1,0:T(8,128)S(1)} %collective-permute-done.13.refs_2_, ...), custom_call_target="tpu_custom_call", output_to_operand_aliasing={{2}: (4, {})} | custom-call | flops 1024 | bytes 4096 | tf_op jit(solution)/shard_map/pallas_call | solution.py:48
  167.1 3.3 %collective-permute-start.18 = (f32[32,2560]{1,0:T(8,128)}, f32[32,2560]{1,0:T(8,128)S(1)}, u32[]{:S(2)}, u32[]{:S(2)}) collective-permute-start(f32[32,2560]{1,0:T(8,128)} %get-tuple-element.123), channel_id=1, source_target_pairs={{0,48},{16,0},{32,16},{48,32},{1,49},{17,1},{33,17},{49,33},{2,50}... | collective-permute-start | bytes 983048 | tf_op jit(solution)/shard_map/ppermute | solution.py:279
  178.0 3.8 %shard_map.76 = (f32[2,64,2560]{2,1,0:T(8,128)}, f32[8,16,1]{2,1,0:T(8,128)S(1)}, f32[6656,2560]{1,0:T(8,128)}) custom-call(s32[4]{0:T(128)S(1)} %pad_add_fusion.2.refs_0_, f32[64,2560]{1,0:T(8,128)} %get-tuple-element.135.refs_1_, f32[64,2560]{1,0:T(8,128)S(1)} %get-tuple-element.136.refs_2_, ...), custom_call_target="tpu_custom_call", output_to_operand_aliasing={{2}: (4, {})} | custom-call | flops 1024 | bytes 4096 | tf_op jit(solution)/shard_map/pallas_call | solution.py:48
  183.4 2.1 %collective-permute-done.22.refs_2_ = f32[32,2560]{1,0:T(8,128)S(1)} collective-permute-done((f32[32,2560]{1,0:T(8,128)S(1)}, f32[32,2560]{1,0:T(8,128)S(1)}, u32[]{:S(2)}, u32[]{:S(2)}) %collective-permute-start.22) | collective-permute-done | bytes 327712 | tf_op jit(solution)/shard_map/ppermute | solution.py:279
  187.2 3.9 %collective-permute-start.24 = (f32[2,64]{1,0:T(2,128)S(1)}, f32[2,64]{1,0:T(2,128)S(1)}, u32[]{:S(2)}, u32[]{:S(2)}) collective-permute-start(f32[2,64]{1,0:T(2,128)S(1)} %reshape.27), channel_id=1, source_target_pairs={{0,1},{1,0},{2,3},{3,2},{4,5},{5,4},{6,7},{7,6},{8,9},{9,8},{10,11... | collective-permute-start | bytes 1544 | tf_op jit(solution)/shard_map/bands/ppermute | solution.py:279
  192.6 3.0 %collective-permute-start.25 = (f32[2,64]{1,0:T(2,128)S(1)}, f32[2,64]{1,0:T(2,128)S(1)}, u32[]{:S(2)}, u32[]{:S(2)}) collective-permute-start(f32[2,64]{1,0:T(2,128)S(1)} %add.193), channel_id=1, source_target_pairs={{0,4},{2,6},{4,0},{6,2},{1,5},{3,7},{5,1},{7,3},{8,12},{10,14},{12... | collective-permute-start | bytes 1544 | tf_op jit(solution)/shard_map/bands/ppermute | solution.py:279
  196.2 2.7 %collective-permute-start.27 = (f32[2,64]{1,0:T(2,128)S(1)}, f32[2,64]{1,0:T(2,128)S(1)}, u32[]{:S(2)}, u32[]{:S(2)}) collective-permute-start(f32[2,64]{1,0:T(2,128)S(1)} %add.193), channel_id=1, source_target_pairs={{0,6},{2,0},{4,2},{6,4},{1,7},{3,1},{5,3},{7,5},{8,14},{10,8},{12,... | collective-permute-start | bytes 1544 | tf_op jit(solution)/shard_map/bands/ppermute | solution.py:279
  (82 shorter events, 23.2 us)
Async XLA Ops:
  0.6 33.7 %collective-permute-start.3 = (f32[1280,2560]{1,0:T(8,128)}, f32[1280,2560]{1,0:T(8,128)}, u32[]{:S(2)}, u32[]{:S(2)}) collective-permute-start(f32[1280,2560]{1,0:T(8,128)} %refs_0_.1), channel_id=1, source_target_pairs={{0,8},{8,0},{1,9},{9,1},{2,10},{10,2},{3,11},{11,3},{4,12},{12,4},... | collective-permute-start | bytes 39321608 | tf_op jit(solution)/shard_map/ppermute | solution.py:279
  3.7 23.7 %all-to-all-start = ((f32[8,16,2560]{2,1,0:T(8,128)}), f32[8,16,2560]{2,1,0:T(8,128)S(1)}, u32[]{:S(2)}, u32[]{:S(2)}) async-start(f32[8,16,2560]{2,1,0:T(8,128)} %get-tuple-element.74), calls=%async_computation | async-start | bytes 2621440 | tf_op jit(solution)/shard_map/rows_to_their_plane_waves/all_to_all | solution.py:303
  9.2 4.7 %copy-start.2 = (f32[1280,2560]{1,0:T(8,128)S(1)}, f32[1280,2560]{1,0:T(8,128)}, u32[]{:S(2)}) copy-start(f32[1280,2560]{1,0:T(8,128)} %refs_0_.1) | copy-start | bytes 39321604
  27.5 34.9 %collective-permute-start = (f32[8,16,2560]{2,1,0:T(8,128)S(1)}, f32[8,16,2560]{2,1,0:T(8,128)}, u32[]{:S(2)}, u32[]{:S(2)}) collective-permute-start(f32[8,16,2560]{2,1,0:T(8,128)S(1)} %get-tuple-element.77.refs_1_), channel_id=1, source_target_pairs={{0,1},{1,0},{2,3},{3,2},{4,5},{5,4},{6,7},{7,6},{8,9},{9,8},{10,11... | collective-permute-start | bytes 3932168 | tf_op jit(solution)/shard_map/near_chunks/ppermute | solution.py:279
  30.2 32.2 %collective-permute-start.1 = (f32[8,16,2560]{2,1,0:T(8,128)S(1)}, f32[8,16,2560]{2,1,0:T(8,128)}, u32[]{:S(2)}, u32[]{:S(2)}) collective-permute-start(f32[8,16,2560]{2,1,0:T(8,128)S(1)} %get-tuple-element.77.refs_1_), channel_id=1, source_target_pairs={{0,6},{2,0},{4,2},{6,4},{1,7},{3,1},{5,3},{7,5},{8,14},{10,8},{12,... | collective-permute-start | bytes 3932168 | tf_op jit(solution)/shard_map/near_chunks/ppermute | solution.py:279
  34.2 31.1 %collective-permute-start.2 = (f32[8,16,2560]{2,1,0:T(8,128)S(1)}, f32[8,16,2560]{2,1,0:T(8,128)S(1)}, u32[]{:S(2)}, u32[]{:S(2)}) collective-permute-start(f32[8,16,2560]{2,1,0:T(8,128)S(1)} %get-tuple-element.77.refs_1_), channel_id=1, source_target_pairs={{0,2},{2,4},{4,6},{6,0},{1,3},{3,5},{5,7},{7,1},{8,10},{10,12},{12... | collective-permute-start | bytes 3932168 | tf_op jit(solution)/shard_map/near_chunks/ppermute | solution.py:279
  52.4 10.0 %collective-permute-start.4 = (f32[32,2560]{1,0:T(8,128)S(1)}, f32[32,2560]{1,0:T(8,128)S(1)}, u32[]{:S(2)}, u32[]{:S(2)}) collective-permute-start(f32[32,2560]{1,0:T(8,128)S(1)} %get-tuple-element.80), channel_id=1, source_target_pairs={{0,16},{16,32},{32,48},{48,0},{1,17},{17,33},{33,49},{49,1},{2,18}... | collective-permute-start | bytes 983048 | tf_op jit(solution)/shard_map/ppermute | solution.py:279
  53.2 9.2 %collective-permute-start.5 = (f32[32,2560]{1,0:T(8,128)S(1)}, f32[32,2560]{1,0:T(8,128)S(1)}, u32[]{:S(2)}, u32[]{:S(2)}) collective-permute-start(f32[32,2560]{1,0:T(8,128)S(1)} %get-tuple-element.81), channel_id=1, source_target_pairs={{0,48},{16,0},{32,16},{48,32},{1,49},{17,1},{33,17},{49,33},{2,50}... | collective-permute-start | bytes 983048 | tf_op jit(solution)/shard_map/ppermute | solution.py:279
  65.3 30.7 %collective-permute-start.6 = (f32[8,16,2560]{2,1,0:T(8,128)}, f32[8,16,2560]{2,1,0:T(8,128)S(1)}, u32[]{:S(2)}, u32[]{:S(2)}) collective-permute-start(f32[8,16,2560]{2,1,0:T(8,128)} %get-tuple-element.84.refs_2_), channel_id=1, source_target_pairs={{0,1},{1,0},{2,3},{3,2},{4,5},{5,4},{6,7},{7,6},{8,9},{9,8},{10,11... | collective-permute-start | bytes 3932168 | tf_op jit(solution)/shard_map/far_chunks/ppermute | solution.py:279
  66.1 30.1 %collective-permute-start.7 = (f32[8,16,2560]{2,1,0:T(8,128)}, f32[8,16,2560]{2,1,0:T(8,128)S(1)}, u32[]{:S(2)}, u32[]{:S(2)}) collective-permute-start(f32[8,16,2560]{2,1,0:T(8,128)} %get-tuple-element.85.refs_1_), channel_id=1, source_target_pairs={{0,2},{2,4},{4,6},{6,0},{1,3},{3,5},{5,7},{7,1},{8,10},{10,12},{12... | collective-permute-start | bytes 3932168 | tf_op jit(solution)/shard_map/far_chunks/ppermute | solution.py:279
  66.1 30.1 %collective-permute-start.8 = (f32[8,16,2560]{2,1,0:T(8,128)}, f32[8,16,2560]{2,1,0:T(8,128)S(1)}, u32[]{:S(2)}, u32[]{:S(2)}) collective-permute-start(f32[8,16,2560]{2,1,0:T(8,128)} %get-tuple-element.84.refs_2_), channel_id=1, source_target_pairs={{0,6},{2,0},{4,2},{6,4},{1,7},{3,1},{5,3},{7,5},{8,14},{10,8},{12,... | collective-permute-start | bytes 3932168 | tf_op jit(solution)/shard_map/far_chunks/ppermute | solution.py:279
  90.8 25.8 %collective-permute-start.11 = (f32[112,2560]{1,0:T(8,128)S(1)}, f32[112,2560]{1,0:T(8,128)S(1)}, u32[]{:S(2)}, u32[]{:S(2)}) collective-permute-start(f32[112,2560]{1,0:T(8,128)S(1)} %get-tuple-element.100), channel_id=1, source_target_pairs={{0,16},{16,32},{32,48},{48,0},{1,17},{17,33},{33,49},{49,1},{2,18}... | collective-permute-start | bytes 3440648 | tf_op jit(solution)/shard_map/ppermute | solution.py:279
  91.2 25.3 %collective-permute-start.12 = (f32[112,2560]{1,0:T(8,128)S(1)}, f32[112,2560]{1,0:T(8,128)S(1)}, u32[]{:S(2)}, u32[]{:S(2)}) collective-permute-start(f32[112,2560]{1,0:T(8,128)S(1)} %get-tuple-element.101), channel_id=1, source_target_pairs={{0,48},{16,0},{32,16},{48,32},{1,49},{17,1},{33,17},{49,33},{2,50}... | collective-permute-start | bytes 3440648 | tf_op jit(solution)/shard_map/ppermute | solution.py:279
  96.3 19.5 %collective-permute-start.10 = (f32[8,8,2560]{2,1,0:T(8,128)S(1)}, f32[8,8,2560]{2,1,0:T(8,128)S(1)}, u32[]{:S(2)}, u32[]{:S(2)}) collective-permute-start(f32[8,8,2560]{2,1,0:T(8,128)S(1)} %slice.13), channel_id=1, source_target_pairs={{0,6},{2,0},{4,2},{6,4},{1,7},{3,1},{5,3},{7,5},{8,14},{10,8},{12,... | collective-permute-start | bytes 1966088 | tf_op jit(solution)/shard_map/last_chunk/ppermute | solution.py:279
  99.4 16.4 %collective-permute-start.9 = (f32[8,8,2560]{2,1,0:T(8,128)S(1)}, f32[8,8,2560]{2,1,0:T(8,128)S(1)}, u32[]{:S(2)}, u32[]{:S(2)}) collective-permute-start(f32[8,8,2560]{2,1,0:T(8,128)S(1)} %slice.12), channel_id=1, source_target_pairs={{0,2},{2,4},{4,6},{6,0},{1,3},{3,5},{5,7},{7,1},{8,10},{10,12},{12... | collective-permute-start | bytes 1966088 | tf_op jit(solution)/shard_map/last_chunk/ppermute | solution.py:279
  120.1 30.6 %collective-permute-start.15 = (f32[112,2560]{1,0:T(8,128)}, f32[112,2560]{1,0:T(8,128)}, u32[]{:S(2)}, u32[]{:S(2)}) collective-permute-start(f32[112,2560]{1,0:T(8,128)} %get-tuple-element.113), channel_id=1, source_target_pairs={{0,16},{16,32},{32,48},{48,0},{1,17},{17,33},{33,49},{49,1},{2,18}... | collective-permute-start | bytes 3440648 | tf_op jit(solution)/shard_map/ppermute | solution.py:279
  120.1 30.5 %collective-permute-start.16 = (f32[112,2560]{1,0:T(8,128)}, f32[112,2560]{1,0:T(8,128)}, u32[]{:S(2)}, u32[]{:S(2)}) collective-permute-start(f32[112,2560]{1,0:T(8,128)} %get-tuple-element.114), channel_id=1, source_target_pairs={{0,48},{16,0},{32,16},{48,32},{1,49},{17,1},{33,17},{49,33},{2,50}... | collective-permute-start | bytes 3440648 | tf_op jit(solution)/shard_map/ppermute | solution.py:279
  123.4 31.5 %all-to-all-start.1 = ((f32[8,16,2560]{2,1,0:T(8,128)}), f32[8,16,2560]{2,1,0:T(8,128)S(1)}, u32[]{:S(2)}, u32[]{:S(2)}) async-start(f32[8,16,2560]{2,1,0:T(8,128)} %get-tuple-element.115), calls=%async_computation.1 | async-start | bytes 2621440 | tf_op jit(solution)/shard_map/second_index/all_to_all | solution.py:348
  147.4 17.7 %collective-permute-start.13 = (f32[64,2560]{1,0:T(8,128)}, f32[64,2560]{1,0:T(8,128)S(1)}, u32[]{:S(2)}, u32[]{:S(2)}) collective-permute-start(f32[64,2560]{1,0:T(8,128)} %get-tuple-element.110), channel_id=1, source_target_pairs={{0,16},{16,32},{32,48},{48,0},{1,17},{17,33},{33,49},{49,1},{2,18}... | collective-permute-start | bytes 1966088 | tf_op jit(solution)/shard_map/ppermute | solution.py:279
  147.4 17.6 %collective-permute-start.14 = (f32[64,2560]{1,0:T(8,128)}, f32[64,2560]{1,0:T(8,128)}, u32[]{:S(2)}, u32[]{:S(2)}) collective-permute-start(f32[64,2560]{1,0:T(8,128)} %get-tuple-element.111), channel_id=1, source_target_pairs={{0,48},{16,0},{32,16},{48,32},{1,49},{17,1},{33,17},{49,33},{2,50}... | collective-permute-start | bytes 1966088 | tf_op jit(solution)/shard_map/ppermute | solution.py:279
  154.0 19.8 %collective-permute-start.19 = (f32[64,2560]{1,0:T(8,128)}, f32[64,2560]{1,0:T(8,128)S(1)}, u32[]{:S(2)}, u32[]{:S(2)}) collective-permute-start(f32[64,2560]{1,0:T(8,128)} %get-tuple-element.124), channel_id=1, source_target_pairs={{0,64},{64,0},{1,65},{65,1},{2,66},{66,2},{3,67},{67,3},{4,68},{68... | collective-permute-start | bytes 1966088 | tf_op jit(solution)/shard_map/ppermute | solution.py:279
  158.0 13.4 %collective-permute-start.20 = (f32[32,2560]{1,0:T(8,128)}, f32[32,2560]{1,0:T(8,128)S(1)}, u32[]{:S(2)}, u32[]{:S(2)}) collective-permute-start(f32[32,2560]{1,0:T(8,128)} %get-tuple-element.125), channel_id=1, source_target_pairs={{0,16},{16,32},{32,48},{48,0},{1,17},{17,33},{33,49},{49,1},{2,18}... | collective-permute-start | bytes 983048 | tf_op jit(solution)/shard_map/ppermute | solution.py:279
  158.1 13.4 %collective-permute-start.21 = (f32[32,2560]{1,0:T(8,128)S(1)}, f32[32,2560]{1,0:T(8,128)S(1)}, u32[]{:S(2)}, u32[]{:S(2)}) collective-permute-start(f32[32,2560]{1,0:T(8,128)S(1)} %get-tuple-element.126), channel_id=1, source_target_pairs={{0,48},{16,0},{32,16},{48,32},{1,49},{17,1},{33,17},{49,33},{2,50}... | collective-permute-start | bytes 983048 | tf_op jit(solution)/shard_map/ppermute | solution.py:279
  167.1 8.5 %collective-permute-start.17 = (f32[32,2560]{1,0:T(8,128)}, f32[32,2560]{1,0:T(8,128)S(1)}, u32[]{:S(2)}, u32[]{:S(2)}) collective-permute-start(f32[32,2560]{1,0:T(8,128)} %get-tuple-element.122), channel_id=1, source_target_pairs={{0,16},{16,32},{32,48},{48,0},{1,17},{17,33},{33,49},{49,1},{2,18}... | collective-permute-start | bytes 983048 | tf_op jit(solution)/shard_map/ppermute | solution.py:279
  167.1 8.5 %collective-permute-start.18 = (f32[32,2560]{1,0:T(8,128)}, f32[32,2560]{1,0:T(8,128)S(1)}, u32[]{:S(2)}, u32[]{:S(2)}) collective-permute-start(f32[32,2560]{1,0:T(8,128)} %get-tuple-element.123), channel_id=1, source_target_pairs={{0,48},{16,0},{32,16},{48,32},{1,49},{17,1},{33,17},{49,33},{2,50}... | collective-permute-start | bytes 983048 | tf_op jit(solution)/shard_map/ppermute | solution.py:279
  172.9 9.1 %collective-permute-start.23 = (f32[32,2560]{1,0:T(8,128)S(1)}, f32[32,2560]{1,0:T(8,128)S(1)}, u32[]{:S(2)}, u32[]{:S(2)}) collective-permute-start(f32[32,2560]{1,0:T(8,128)S(1)} %get-tuple-element.134), channel_id=1, source_target_pairs={{0,64},{64,0},{1,65},{65,1},{2,66},{66,2},{3,67},{67,3},{4,68},{68... | collective-permute-start | bytes 983048 | tf_op jit(solution)/shard_map/ppermute | solution.py:279
  177.1 8.4 %collective-permute-start.22 = (f32[32,2560]{1,0:T(8,128)S(1)}, f32[32,2560]{1,0:T(8,128)S(1)}, u32[]{:S(2)}, u32[]{:S(2)}) collective-permute-start(f32[32,2560]{1,0:T(8,128)S(1)} %get-tuple-element.131), channel_id=1, source_target_pairs={{0,64},{64,0},{1,65},{65,1},{2,66},{66,2},{3,67},{67,3},{4,68},{68... | collective-permute-start | bytes 983048 | tf_op jit(solution)/shard_map/ppermute | solution.py:279
  185.5 13.3 %copy-start.8 = (s32[64]{0:T(128)S(1)}, s32[64]{0:T(128)}, u32[]{:S(2)}) copy-start(s32[64]{0:T(128)} %param.6) | copy-start | bytes 772
  187.2 5.4 %collective-permute-start.24 = (f32[2,64]{1,0:T(2,128)S(1)}, f32[2,64]{1,0:T(2,128)S(1)}, u32[]{:S(2)}, u32[]{:S(2)}) collective-permute-start(f32[2,64]{1,0:T(2,128)S(1)} %reshape.27), channel_id=1, source_target_pairs={{0,1},{1,0},{2,3},{3,2},{4,5},{5,4},{6,7},{7,6},{8,9},{9,8},{10,11... | collective-permute-start | bytes 1544 | tf_op jit(solution)/shard_map/bands/ppermute | solution.py:279
  192.6 6.2 %collective-permute-start.25 = (f32[2,64]{1,0:T(2,128)S(1)}, f32[2,64]{1,0:T(2,128)S(1)}, u32[]{:S(2)}, u32[]{:S(2)}) collective-permute-start(f32[2,64]{1,0:T(2,128)S(1)} %add.193), channel_id=1, source_target_pairs={{0,4},{2,6},{4,0},{6,2},{1,5},{3,7},{5,1},{7,3},{8,12},{10,14},{12... | collective-permute-start | bytes 1544 | tf_op jit(solution)/shard_map/bands/ppermute | solution.py:279
  195.6 4.8 %collective-permute-start.26 = (f32[2,64]{1,0:T(2,128)S(1)}, f32[2,64]{1,0:T(2,128)S(1)}, u32[]{:S(2)}, u32[]{:S(2)}) collective-permute-start(f32[2,64]{1,0:T(2,128)S(1)} %add.193), channel_id=1, source_target_pairs={{0,2},{2,4},{4,6},{6,0},{1,3},{3,5},{5,7},{7,1},{8,10},{10,12},{12... | collective-permute-start | bytes 1544 | tf_op jit(solution)/shard_map/bands/ppermute | solution.py:279
  196.2 4.2 %collective-permute-start.27 = (f32[2,64]{1,0:T(2,128)S(1)}, f32[2,64]{1,0:T(2,128)S(1)}, u32[]{:S(2)}, u32[]{:S(2)}) collective-permute-start(f32[2,64]{1,0:T(2,128)S(1)} %add.193), channel_id=1, source_target_pairs={{0,6},{2,0},{4,2},{6,4},{1,7},{3,1},{5,3},{7,5},{8,14},{10,8},{12,... | collective-permute-start | bytes 1544 | tf_op jit(solution)/shard_map/bands/ppermute | solution.py:279
  (7 other events, 19.7 us)
